TPU v7x, 32 devices: a whole 2x2x4 slice. The times are simulated.
32 devices in a mesh: dev: 32 (over z, y, x, core).
Axes of the slice: x: 2, y: 2, z: 4, core: 2. Of those that a mesh axis runs over, the one named last changes fastest.
Arguments:
- tokens: bfloat16 [16384, 1280], P('dev'), may hold values from -6 to 6
- lengths: int32 [16], replicated, may hold values from 256 to 1024, as said below
- out_grad: bfloat16 [16384, 1280], P('dev'), may hold values from -6 to 6
- first_gain: bfloat16 [1280], P('dev'), may hold values from 0.5 to 1.5
- first_shift: bfloat16 [1280], P('dev'), may hold values from -3 to 3
- query_weight: bfloat16 [1280, 1280], P('dev'), may hold values from -0.15625 to 0.15625
- query_bias: bfloat16 [1280], P('dev'), may hold values from -3 to 3
- key_weight: bfloat16 [1280, 1280], P('dev'), may hold values from -0.15625 to 0.15625
- value_weight: bfloat16 [1280, 1280], P('dev'), may hold values from -0.15625 to 0.15625
- value_bias: bfloat16 [1280], P('dev'), may hold values from -0.29882812 to 0.29882812
- proj_weight: bfloat16 [1280, 1280], P('dev'), may hold values from -2.5 to 2.5
- proj_bias: bfloat16 [1280], P('dev'), may hold values from -3 to 3
- mid_gain: bfloat16 [1280], P('dev'), may hold values from 0.5 to 1.5
- mid_shift: bfloat16 [1280], P('dev'), may hold values from -3 to 3
- up_weight: bfloat16 [1280, 5120], P('dev'), may hold values from -0.15625 to 0.15625
- up_bias: bfloat16 [5120], P('dev'), may hold values from -3 to 3
- down_weight: bfloat16 [5120, 1280], P('dev'), may hold values from -0.078125 to 0.078125
- down_bias: bfloat16 [1280], P('dev'), may hold values from -3 to 3
Outputs:
- output: bfloat16 [16384, 1280], P('dev')
- input_grad: bfloat16 [16384, 1280], P('dev')
- first_gain_grad: float32 [1280], P('dev')
- first_shift_grad: float32 [1280], P('dev')
- query_weight_grad: float32 [1280, 1280], P('dev')
- query_bias_grad: float32 [1280], P('dev')
- key_weight_grad: float32 [1280, 1280], P('dev')
- value_weight_grad: float32 [1280, 1280], P('dev')
- value_bias_grad: float32 [1280], P('dev')
- proj_weight_grad: float32 [1280, 1280], P('dev')
- proj_bias_grad: float32 [1280], P('dev')
- mid_gain_grad: float32 [1280], P('dev')
- mid_shift_grad: float32 [1280], P('dev')
- up_weight_grad: float32 [1280, 5120], P('dev')
- up_bias_grad: float32 [5120], P('dev')
- down_weight_grad: float32 [5120, 1280], P('dev')
- down_bias_grad: float32 [1280], P('dev')
Inputs may be any that keep to these rules, and one draw needn't show every extreme that they name: Clip c holds rows c * 1024 to (c + 1) * 1024 - 1, of which the first lengths[c] are real; in every draw some clip is full.
All inputs are finite; a program needn't handle non-finite values.
Results may differ from a plain program's by a relative error of at most 0.012.
Values may be sent and summed in bfloat16 or wider, within the bound.
No kernel may reach another device: no remote copies, remote signals or barrier semaphores. Data moves between devices by JAX's collectives and lax.ppermute only.
A program may use at most 320 MiB of HBM per device.

v0:
```python
import jax
import jax.numpy as jnp
from jax import lax
from jax.sharding import PartitionSpec as P

H = 16
HD = 80
SPAN = 2


EPS = 1e-05
NEG = -1e30


def shifted(value, axis, steps):
    count = lax.axis_size(axis)
    first, last = (max(0, -steps), min(count, count - steps))
    return lax.ppermute(value, axis, [(source, source + steps) for source in range(first, last)])


def layer_norm(values, gain, shift):
    center = values - jnp.mean(values, axis=-1, keepdims=True)
    spread = jnp.mean(center * center, axis=-1, keepdims=True)
    return center * lax.rsqrt(spread + EPS) * gain + shift


def gelu_exact(values):
    return jax.nn.gelu(values, approximate=False)


def matmul(left, right):
    return jnp.dot(left, right, preferred_element_type=jnp.float32)


def dot_rows(left, right):
    return lax.dot_general(
        left, right, (((0,), (0,)), ((), ())), preferred_element_type=jnp.float32
    )


def dot_cols(left, right):
    return lax.dot_general(
        left, right, (((1,), (1,)), ((), ())), preferred_element_type=jnp.float32
    )


def split_heads(array):
    return array.reshape(array.shape[0], H, HD).transpose(1, 0, 2)


def merge_heads(array):
    return array.transpose(1, 0, 2).reshape(array.shape[1], H * HD)


def from_peer(block, offset):
    return shifted(block, "dev", offset)


def to_peer(block, offset):
    return shifted(block.astype(jnp.bfloat16), "dev", offset).astype(block.dtype)


def body(
    tokens,
    lengths,
    out_grad,
    first_gain,
    first_shift,
    query_weight,
    query_bias,
    key_weight,
    value_weight,
    value_bias,
    proj_weight,
    proj_bias,
    mid_gain,
    mid_shift,
    up_weight,
    up_bias,
    down_weight,
    down_bias,
):
    shards = (
        first_gain,
        first_shift,
        query_weight,
        query_bias,
        key_weight,
        value_weight,
        value_bias,
        proj_weight,
        proj_bias,
        mid_gain,
        mid_shift,
        up_weight,
        up_bias,
        down_weight,
        down_bias,
    )
    gathered = (
        lax.all_gather(shards[0], "dev", axis=0, tiled=True),
        lax.all_gather(shards[1], "dev", axis=0, tiled=True),
        lax.all_gather(shards[2], "dev", axis=0, tiled=True),
        lax.all_gather(shards[3], "dev", axis=0, tiled=True),
        lax.all_gather(shards[4], "dev", axis=0, tiled=True),
        lax.all_gather(shards[5], "dev", axis=0, tiled=True),
        lax.all_gather(shards[6], "dev", axis=0, tiled=True),
        lax.all_gather(shards[7], "dev", axis=0, tiled=True),
        lax.all_gather(shards[8], "dev", axis=0, tiled=True),
        lax.all_gather(shards[9], "dev", axis=0, tiled=True),
        lax.all_gather(shards[10], "dev", axis=0, tiled=True),
        lax.all_gather(shards[11], "dev", axis=0, tiled=True),
        lax.all_gather(shards[12], "dev", axis=0, tiled=True),
        lax.all_gather(shards[13], "dev", axis=0, tiled=True),
        lax.all_gather(shards[14], "dev", axis=0, tiled=True),
    )
    (
        pre_gain,
        pre_shift,
        w_query,
        b_query,
        w_key,
        w_value,
        b_value,
        w_proj,
        b_proj,
        mid_gain_all,
        mid_shift_all,
        w_up,
        b_up,
        w_down,
        b_down,
    ) = gathered
    rows = tokens.shape[0]
    width = tokens.shape[1]
    scale = HD ** (-0.5)
    position = lax.axis_index("dev")
    group_pos = position % SPAN
    clip_length = jnp.sum(jnp.where(jnp.arange(lengths.shape[0]) == position // SPAN, lengths, 0))
    key_live = jnp.arange(SPAN * rows) < clip_length
    row_live = group_pos * rows + jnp.arange(rows) < clip_length
    offsets = [step for step in range(1 - SPAN, SPAN) if step != 0]
    inputs = tokens.astype(jnp.float32)
    normed, pre_back = jax.vjp(
        layer_norm, inputs, pre_gain.astype(jnp.float32), pre_shift.astype(jnp.float32)
    )
    normed_low = normed.astype(jnp.bfloat16)
    queries = (matmul(normed_low, w_query) + b_query.astype(jnp.float32)).astype(jnp.bfloat16)
    keys = matmul(normed_low, w_key).astype(jnp.bfloat16)
    values = (matmul(normed_low, w_value) + b_value.astype(jnp.float32)).astype(jnp.bfloat16)
    local_pair = jnp.concatenate([keys, values], axis=1)
    arrived = {0: local_pair}
    for offset in offsets:
        arrived[offset] = from_peer(local_pair, offset)
    blocks = []
    for slot in range(SPAN):
        block = jnp.zeros_like(local_pair)
        for offset in [0] + offsets:
            block = jnp.where(group_pos - offset == slot, arrived[offset], block)
        blocks.append(block)
    group_pair = jnp.concatenate(blocks, axis=0)
    query_heads = split_heads(queries)
    key_heads = split_heads(group_pair[:, :width])
    value_heads = split_heads(group_pair[:, width:])

    def head_forward(operands):
        query_head, key_head, value_head = operands
        scores = jnp.where(key_live[None, :], dot_cols(query_head, key_head) * scale, NEG)
        top = jnp.max(scores, axis=1, keepdims=True)
        weights = jnp.exp(scores - top)
        total = jnp.sum(weights, axis=1, keepdims=True)
        probs_low = (weights / total).astype(jnp.bfloat16)
        return (matmul(probs_low, value_head).astype(jnp.bfloat16), (top + jnp.log(total))[:, 0])

    attended_heads, log_totals = lax.map(head_forward, (query_heads, key_heads, value_heads))
    attended = merge_heads(attended_heads)
    mid = inputs + matmul(attended, w_proj) + b_proj.astype(jnp.float32)
    mid_normed, mid_back = jax.vjp(
        layer_norm, mid, mid_gain_all.astype(jnp.float32), mid_shift_all.astype(jnp.float32)
    )
    mid_low = mid_normed.astype(jnp.bfloat16)
    pre_act = matmul(mid_low, w_up) + b_up.astype(jnp.float32)
    activ, gelu_back = jax.vjp(gelu_exact, pre_act)
    activ_low = activ.astype(jnp.bfloat16)
    output = (mid + matmul(activ_low, w_down) + b_down.astype(jnp.float32)).astype(jnp.bfloat16)
    again = (
        lax.all_gather(shards[0], "dev", axis=0, tiled=True),
        lax.all_gather(shards[1], "dev", axis=0, tiled=True),
        lax.all_gather(shards[2], "dev", axis=0, tiled=True),
        lax.all_gather(shards[3], "dev", axis=0, tiled=True),
        lax.all_gather(shards[4], "dev", axis=0, tiled=True),
        lax.all_gather(shards[5], "dev", axis=0, tiled=True),
        lax.all_gather(shards[6], "dev", axis=0, tiled=True),
        lax.all_gather(shards[7], "dev", axis=0, tiled=True),
        lax.all_gather(shards[8], "dev", axis=0, tiled=True),
        lax.all_gather(shards[9], "dev", axis=0, tiled=True),
        lax.all_gather(shards[10], "dev", axis=0, tiled=True),
        lax.all_gather(shards[11], "dev", axis=0, tiled=True),
        lax.all_gather(shards[12], "dev", axis=0, tiled=True),
        lax.all_gather(shards[13], "dev", axis=0, tiled=True),
        lax.all_gather(shards[14], "dev", axis=0, tiled=True),
    )
    (
        unused_gain,
        unused_shift,
        w_query,
        unused_bias,
        w_key,
        w_value,
        unused_value,
        w_proj,
        unused_proj,
        unused_mid,
        unused_midb,
        w_up,
        unused_up,
        w_down,
        unused_down,
    ) = again
    grad_low = jnp.where(row_live[:, None], out_grad, jnp.zeros_like(out_grad))
    grad_full = grad_low.astype(jnp.float32)
    down_w_grad = dot_rows(activ_low, grad_low)
    down_b_grad = jnp.sum(grad_full, axis=0)
    activ_grad = dot_cols(grad_low, w_down)
    pre_grad = gelu_back(activ_grad)[0].astype(jnp.bfloat16)
    up_w_grad = dot_rows(mid_low, pre_grad)
    up_b_grad = jnp.sum(pre_grad.astype(jnp.float32), axis=0)
    mid_in_grad, mid_gain_grad, mid_shift_grad = mid_back(dot_cols(pre_grad, w_up))
    mid_grad = grad_full + mid_in_grad
    branch_grad = mid_grad.astype(jnp.bfloat16)
    proj_w_grad = dot_rows(attended, branch_grad)
    proj_b_grad = jnp.sum(branch_grad.astype(jnp.float32), axis=0)
    attended_grad = dot_cols(branch_grad, w_proj).astype(jnp.bfloat16)

    def head_backward(operands):
        query_head, key_head, value_head, out_head_grad, log_total = operands
        scores = jnp.where(key_live[None, :], dot_cols(query_head, key_head) * scale, NEG)
        probs = jnp.exp(scores - log_total[:, None])
        prob_grad = dot_cols(out_head_grad, value_head)
        inner = jnp.sum(probs * prob_grad, axis=1, keepdims=True)
        score_grad = (probs * (prob_grad - inner)).astype(jnp.bfloat16)
        query_part = (matmul(score_grad, key_head) * scale).astype(jnp.bfloat16)
        key_part = dot_rows(score_grad, query_head) * scale
        value_part = dot_rows(probs.astype(jnp.bfloat16), out_head_grad)
        return (query_part, key_part, value_part)

    query_parts, key_parts, value_parts = lax.map(
        head_backward, (query_heads, key_heads, value_heads, split_heads(attended_grad), log_totals)
    )
    query_grad = merge_heads(query_parts)
    pair_partial = jnp.concatenate([merge_heads(key_parts), merge_heads(value_parts)], axis=1)
    own_pair = lax.dynamic_slice_in_dim(pair_partial, group_pos * rows, rows, 0)
    for offset in offsets:
        target = jnp.clip(group_pos + offset, 0, SPAN - 1)
        sent = lax.dynamic_slice_in_dim(pair_partial, target * rows, rows, 0)
        received = to_peer(sent, offset)
        inside = (group_pos - offset >= 0) & (group_pos - offset < SPAN)
        own_pair = own_pair + jnp.where(inside, received, 0.0)
    pair_grad = own_pair.astype(jnp.bfloat16)
    key_grad = pair_grad[:, :width]
    value_grad = pair_grad[:, width:]
    normed_grad = (
        dot_cols(query_grad, w_query) + dot_cols(key_grad, w_key) + dot_cols(value_grad, w_value)
    )
    query_w_grad = dot_rows(normed_low, query_grad)
    query_b_grad = jnp.sum(query_grad.astype(jnp.float32), axis=0)
    key_w_grad = dot_rows(normed_low, key_grad)
    value_w_grad = dot_rows(normed_low, value_grad)
    value_b_grad = jnp.sum(value_grad.astype(jnp.float32), axis=0)
    first_in_grad, pre_gain_grad, pre_shift_grad = pre_back(normed_grad)
    input_grad = (mid_grad + first_in_grad).astype(jnp.bfloat16)
    summed = (
        lax.psum_scatter(pre_gain_grad, "dev", scatter_dimension=0, tiled=True),
        lax.psum_scatter(pre_shift_grad, "dev", scatter_dimension=0, tiled=True),
        lax.psum_scatter(query_w_grad, "dev", scatter_dimension=0, tiled=True),
        lax.psum_scatter(query_b_grad, "dev", scatter_dimension=0, tiled=True),
        lax.psum_scatter(key_w_grad, "dev", scatter_dimension=0, tiled=True),
        lax.psum_scatter(value_w_grad, "dev", scatter_dimension=0, tiled=True),
        lax.psum_scatter(value_b_grad, "dev", scatter_dimension=0, tiled=True),
        lax.psum_scatter(proj_w_grad, "dev", scatter_dimension=0, tiled=True),
        lax.psum_scatter(proj_b_grad, "dev", scatter_dimension=0, tiled=True),
        lax.psum_scatter(mid_gain_grad, "dev", scatter_dimension=0, tiled=True),
        lax.psum_scatter(mid_shift_grad, "dev", scatter_dimension=0, tiled=True),
        lax.psum_scatter(up_w_grad, "dev", scatter_dimension=0, tiled=True),
        lax.psum_scatter(up_b_grad, "dev", scatter_dimension=0, tiled=True),
        lax.psum_scatter(down_w_grad, "dev", scatter_dimension=0, tiled=True),
        lax.psum_scatter(down_b_grad, "dev", scatter_dimension=0, tiled=True),
    )
    (
        gain_one,
        shift_one,
        query_wsum,
        query_bsum,
        key_wsum,
        value_wsum,
        value_bsum,
        proj_wsum,
        proj_bsum,
        gain_two,
        shift_two,
        up_wsum,
        up_bsum,
        down_wsum,
        down_bsum,
    ) = summed
    return (
        output,
        input_grad,
        gain_one,
        shift_one,
        query_wsum,
        query_bsum,
        key_wsum,
        value_wsum,
        value_bsum,
        proj_wsum,
        proj_bsum,
        gain_two,
        shift_two,
        up_wsum,
        up_bsum,
        down_wsum,
        down_bsum,
    )


def solution(mesh):
    placed = (
        P("dev", None),
        P(),
        P("dev", None),
        P("dev"),
        P("dev"),
        P("dev", None),
        P("dev"),
        P("dev", None),
        P("dev", None),
        P("dev"),
        P("dev", None),
        P("dev"),
        P("dev"),
        P("dev"),
        P("dev", None),
        P("dev"),
        P("dev", None),
        P("dev"),
    )
    return jax.shard_map(
        body,
        mesh=mesh,
        in_specs=placed,
        out_specs=(
            P("dev", None),
            P("dev", None),
            P("dev"),
            P("dev"),
            P("dev", None),
            P("dev"),
            P("dev", None),
            P("dev", None),
            P("dev"),
            P("dev", None),
            P("dev"),
            P("dev"),
            P("dev"),
            P("dev", None),
            P("dev"),
            P("dev", None),
            P("dev"),
        ),
        check_vma=False,
    )
```

profile of v0, /device:TPU:0, one launch (start us, length us, event | category | flops | bytes accessed | tf_op | source)
XLA Modules:
  0.0 1718.0 jit_solution(373511739365507249)
XLA Ops:
  18.3 43.4 %all-reduce.19 = (bf16[1280]{0:T(1024)(128)(2,1)S(1)}, bf16[1280]{0:T(1024)(128)(2,1)S(1)}, bf16[1280]{0:T(1024)(128)(2,1)S(1)}, bf16[1280]{0:T(1024)(128)(2,1)S...) all-reduce(bf16[1280]{0:T(1024)(128)(2,1)S(1)} %dynamic-update-slic, ...), channel_id=1, replica_groups=mesh['dev'=32] {'dev'}, use_global_device_ids=true, to_apply=%add.2 | all-reduce | flops 15360 | bytes 61440
  64.3 9.0 all-gather.9.cloned.1.call-done
  73.3 4.0 convolution_convert_fusion.2
  77.3 56.8 %all-gather.11.cloned.1.call-done = bf16[1280,1280]{1,0:T(8,128)(2,1)} async-done(((bf16[40,1280]{1,0:T(8,128)(2,1)}), bf16[1280,1280]{1,0:T(8,128)(2,1)}) %all-gather.11.cloned.1.call-update) | async-done | bytes 3276816 | tf_op jit(solution)/shard_map/all_gather | solution.py:106
  134.0 4.0 fusion.68
  140.0 3.6 collective-permute-start
  146.6 67.9 %all-gather.7.cloned.1.call-done = bf16[1280,1280]{1,0:T(8,128)(2,1)} async-done(((bf16[40,1280]{1,0:T(8,128)(2,1)}), bf16[1280,1280]{1,0:T(8,128)(2,1)}) %all-gather.7.cloned.1.call-update) | async-done | bytes 3276816 | tf_op jit(solution)/shard_map/all_gather | solution.py:103
  214.6 5.0 fusion.67
  221.2 2.6 copy.53
  223.8 4.1 select_select_fusion
  228.0 2.7 pad_maximum_fusion
  230.7 4.5 copy.51
  235.2 5.8 copy.54
  241.0 4.5 copy.52
  245.5 5.8 copy.55
  252.5 82.9 %while.28 = (s32[]{:T(128)}, bf16[16,512,80]{1,2,0:T(8,128)(2,1)}, f32[16,512]{1,0:T(8,128)S(1)}, bf16[16,512,80]{2,1,0:T(8,128)(2,1)}, bf16[16,1024,80]{2,1,0:T...) while((s32[]{:T(128)}, bf16[16,512,80]{1,2,0:T(8,128)(2,1)}, ...), condition=%wide.region_6.7_spmd.clone, body=%wide.region_3.6_spmd.clone.sunk | while | flops 174105088 | bytes 7055461 | solution.py:175
  255.4 2.3 fusion.150
  260.6 2.3 fusion.150
  265.8 2.3 fusion.150
  270.9 2.3 fusion.150
  276.1 2.3 fusion.150
  281.3 2.3 fusion.150
  286.5 2.3 fusion.150
  291.7 2.3 fusion.150
  296.8 2.3 fusion.150
  302.0 2.3 fusion.150
  307.2 2.3 fusion.150
  312.4 2.3 fusion.150
  317.5 2.3 fusion.150
  322.7 2.3 fusion.150
  327.9 2.3 fusion.150
  333.2 2.3 fusion.150
  335.5 4.5 fusion.104
  341.9 33.1 %all-gather.15.cloned.1.call-done = bf16[1280,5120]{1,0:T(8,128)(2,1)} async-done(((bf16[40,5120]{1,0:T(8,128)(2,1)}), bf16[1280,5120]{1,0:T(8,128)(2,1)}) %all-gather.15.cloned.1.call-update) | async-done | bytes 13107216 | tf_op jit(solution)/shard_map/all_gather | solution.py:112
  375.0 34.7 %multiply_convert_fusion.1 = (bf16[512,5120]{1,0:T(8,128)(2,1)}, f32[512,5120]{1,0:T(8,128)}, f32[512,5120]{1,0:T(8,128)}) fusion(f32[5120]{0:T(1024)S(1)} %convert_element_type.122, bf16[1280,5120]{1,0:T(8,128)(2,1)} %all-gather.15.cloned.1.call-done, f32[512,1280]{1,0:T(8,128)} %copy-done.2, f32[1280]{0:T(1024)S(1)} %convert_element_type.120, ...), kind=kOutput, calls=%fused_computation.69 | convolution fusion | flops 6887178240 | bytes 41977856 | tf_op jit(solution)/shard_map/dot_general | solution.py:32
  409.7 64.7 %all-gather.17.cloned.1.call-done = bf16[5120,1280]{1,0:T(8,128)(2,1)} async-done(((bf16[160,1280]{1,0:T(8,128)(2,1)}), bf16[5120,1280]{1,0:T(8,128)(2,1)}) %all-gather.17.cloned.1.call-update) | async-done | bytes 13107216 | tf_op jit(solution)/shard_map/all_gather | solution.py:114
  474.4 20.1 %convert_reduce_fusion = (f32[5120]{0:T(1024)}, bf16[512,5120]{1,0:T(8,128)(2,1)}) fusion(f32[512,5120]{1,0:T(8,128)} %get-tuple-element.252, bf16[5120,1280]{1,0:T(8,128)(2,1)} %all-gather.17.cloned.1.call-done, bf16[512,1280]{1,0:T(8,128)(2,1)} %param.24, pred[512]{0:T(512)(128)(4,1)S(1)} %add_compare_fusion, f32[512,5120]{1,0:T(8,128)} %get-tuple-element.267, ...), kind=kOutput, calls=%fused_computation.67 | convolution fusion | flops 6756101120 | bytes 40673792 | tf_op jit(solution)/shard_map/dot_general | solution.py:42
  494.5 14.8 multiply_reduce_fusion.1
  509.3 2.6 fusion.102
  514.5 4.6 fusion.106
  521.0 4.3 convolution_convert_fusion.1
  525.2 2.6 copy.56
  528.0 153.4 %while.29 = (s32[]{:T(128)}, bf16[16,512,80]{1,2,0:T(8,128)(2,1)S(1)}, f32[16,1024,80]{1,2,0:T(8,128)}, f32[16,1024,80]{1,2,0:T(8,128)}, bf16[16,512,80]{2,1,0:T...) while((s32[]{:T(128)}, ...), condition=%wide.region_13.14_spmd.clone, body=%wide.region_11.13_spmd.clone.sunk | while | flops 424313344 | bytes 17695860 | solution.py:247
  551.5 2.0 fusion.161
  608.9 2.0 fusion.161
  628.1 2.0 fusion.161
  681.5 4.9 fusion.95
  686.5 6.8 fusion.60
  694.6 4.5 collective-permute-start.3
  700.4 2.2 collective-permute-done.3
  702.6 4.6 fusion.58
  708.8 4.9 fusion.82
  713.8 6.3 fusion.79
  720.1 15.6 fusion.89
  737.1 16.2 fusion.91
  755.7 4.4 fusion.105
  760.2 14.0 fusion.69
  776.4 2.4 fusion.100
  780.5 2.4 convert_reduce_fusion.2
  782.9 127.0 %all-reduce.18 = (f32[1280]{0:T(1024)S(1)}, f32[1280]{0:T(1024)S(1)}, f32[1280]{0:T(1024)S(1)}, f32[1280]{0:T(1024)S(1)}, f32[1280]{0:T(1024)S(1)}, /*index=5*/f...) all-reduce(f32[1280]{0:T(1024)S(1)} %get-tuple-element.190, ...), channel_id=2, replica_groups=mesh['dev'=32] {'dev'}, use_global_device_ids=true, to_apply=%region_17.18.clone | all-reduce | flops 15360 | bytes 122880
  915.3 85.4 %reduce-scatter.11.cloned.1.call-done = f32[40,1280]{1,0:T(8,128)} async-done(((f32[1280,1280]{1,0:T(8,128)}), f32[40,1280]{1,0:T(8,128)}) %reduce-scatter.11.cloned.1.call-update) | async-done | bytes 204816 | tf_op jit(solution)/shard_map/reduce_scatter | solution.py:278
  1000.7 144.2 %reduce-scatter.9.cloned.1.call-done = f32[40,1280]{1,0:T(8,128)} async-done(((f32[1280,1280]{1,0:T(8,128)}), f32[40,1280]{1,0:T(8,128)}) %reduce-scatter.9.cloned.1.call-update) | async-done | bytes 204816 | tf_op jit(solution)/shard_map/reduce_scatter | solution.py:277
  1144.9 277.9 %reduce-scatter.15.cloned.1.call-done = f32[40,5120]{1,0:T(8,128)} async-done(((f32[1280,5120]{1,0:T(8,128)}), f32[40,5120]{1,0:T(8,128)}) %reduce-scatter.15.cloned.1.call-update) | async-done | bytes 819216 | tf_op jit(solution)/shard_map/reduce_scatter | solution.py:284
  1422.8 288.0 %reduce-scatter.17.cloned.1.call-done = f32[160,1280]{1,0:T(8,128)} async-done(((f32[5120,1280]{1,0:T(8,128)}), f32[160,1280]{1,0:T(8,128)}) %reduce-scatter.17.cloned.1.call-update) | async-done | bytes 819216 | tf_op jit(solution)/shard_map/reduce_scatter | solution.py:286
  (363 shorter events, 237.5 us)
Async XLA Ops:
  7.2 56.1 %copy-start = (bf16[512,1280]{1,0:T(8,128)(2,1)S(1)}, bf16[512,1280]{1,0:T(8,128)(2,1)}, u32[]{:S(2)}) copy-start(bf16[512,1280]{1,0:T(8,128)(2,1)} %param.22) | copy-start | bytes 3932164
  7.2 66.1 %all-gather.9.cloned.1.call-start = ((), (), s32[]{:S(2)}) async-start(), calls=%async_computation.7 | async-start | bytes 3379200 | tf_op jit(solution)/shard_map/all_gather | solution.py:105
  7.9 126.1 %all-gather.11.cloned.1.call-start = ((), (), s32[]{:S(2)}) async-start(), calls=%async_computation.8 | async-start | bytes 3379200 | tf_op jit(solution)/shard_map/all_gather | solution.py:106
  8.7 205.9 %all-gather.7.cloned.1.call-start = ((), (), s32[]{:S(2)}) async-start(), calls=%async_computation.6 | async-start | bytes 3379200 | tf_op jit(solution)/shard_map/all_gather | solution.py:103
  9.4 326.0 %all-gather.13.cloned.1.call-start = ((), (), s32[]{:S(2)}) async-start(), calls=%async_computation.9 | async-start | bytes 3379200 | tf_op jit(solution)/shard_map/all_gather | solution.py:108
  10.0 365.0 %all-gather.15.cloned.1.call-start = ((), (), s32[]{:S(2)}) async-start(), calls=%async_computation.10 | async-start | bytes 13516800 | tf_op jit(solution)/shard_map/all_gather | solution.py:112
  10.6 463.8 %all-gather.17.cloned.1.call-start = ((), (), s32[]{:S(2)}) async-start(), calls=%async_computation.11 | async-start | bytes 13516800 | tf_op jit(solution)/shard_map/all_gather | solution.py:114
  61.7 152.9 %copy-start.17 = (f32[1280]{0:T(1024)}, f32[1280]{0:T(1024)S(1)}, u32[]{:S(2)}) copy-start(f32[1280]{0:T(1024)S(1)} %convert_element_type.110) | copy-start | bytes 15364
  61.7 152.9 %copy-start.26 = (f32[1280]{0:T(1024)}, f32[1280]{0:T(1024)S(1)}, u32[]{:S(2)}) copy-start(f32[1280]{0:T(1024)S(1)} %convert_element_type.111) | copy-start | bytes 15364
  63.3 151.3 %copy-start.19 = (f32[512]{0:T(512)}, f32[512]{0:T(512)S(1)}, u32[]{:S(2)}) copy-start(f32[512]{0:T(512)S(1)} %broadcast_multiply_fusion.1) | copy-start | bytes 6148
  63.8 0.6 copy-start.24
  64.3 150.2 %copy-start.22 = (f32[512]{0:T(512)}, f32[512]{0:T(512)S(1)}, u32[]{:S(2)}) copy-start(f32[512]{0:T(512)S(1)} %fusion.85) | copy-start | bytes 6148
  77.3 60.8 %copy-start.14 = (bf16[512,1280]{1,0:T(8,128)(2,1)}, bf16[512,1280]{1,0:T(8,128)(2,1)S(1)}, u32[]{:S(2)}) copy-start(bf16[512,1280]{1,0:T(8,128)(2,1)S(1)} %convolution_convert_fusion.2) | copy-start | bytes 3932164
  138.0 1.9 copy-start.15
  138.0 7.3 copy-start.31
  140.0 83.9 %collective-permute-start = (bf16[512,2560]{1,0:T(8,128)(2,1)}, bf16[512,2560]{1,0:T(8,128)(2,1)}, u32[]{:S(2)}, u32[]{:S(2)}) collective-permute-start(bf16[512,2560]{1,0:T(8,128)(2,1)} %pad_maximum_fusion.1), channel_id=1, source_target_pairs={{0,1},{1,2},{2,3},{3,4},{4,5},{5,6},{6,7},{7,8},{8,9},{9,10},{10,1... | collective-permute-start | bytes 7864328 | tf_op jit(solution)/shard_map/ppermute | solution.py:18
  143.6 80.2 %collective-permute-start.1 = (bf16[512,2560]{1,0:T(8,128)(2,1)}, bf16[512,2560]{1,0:T(8,128)(2,1)}, u32[]{:S(2)}, u32[]{:S(2)}) collective-permute-start(bf16[512,2560]{1,0:T(8,128)(2,1)} %pad_maximum_fusion.1), channel_id=1, source_target_pairs={{1,0},{2,1},{3,2},{4,3},{5,4},{6,5},{7,6},{8,7},{9,8},{10,9},{11,1... | collective-permute-start | bytes 7864328 | tf_op jit(solution)/shard_map/ppermute | solution.py:18
  144.9 770.4 %reduce-scatter.13.cloned.1.call-start = ((), (), s32[]{:S(2)}) async-start(), calls=%async_computation.15 | async-start | bytes 6758400 | tf_op jit(solution)/shard_map/reduce_scatter | solution.py:280
  340.0 1.5 copy-start.2
  474.4 20.1 %copy-start.3 = (f32[512,1280]{1,0:T(8,128)S(1)}, f32[512,1280]{1,0:T(8,128)}, u32[]{:S(2)}) copy-start(f32[512,1280]{1,0:T(8,128)} %copy-done.2) | copy-start | bytes 7864324
  509.3 2.6 copy-start.11
  511.9 1.5 copy-start.5
  511.9 2.5 copy-start.8
  513.4 1.1 copy-start.16
  519.0 1.9 copy-start.7
  519.1 396.2 %reduce-scatter.7.cloned.1.call-start = ((), (), s32[]{:S(2)}) async-start(), calls=%async_computation.12 | async-start | bytes 6758400 | tf_op jit(solution)/shard_map/reduce_scatter | solution.py:275
  527.9 153.5 %copy-start.1 = (bf16[512,1280]{1,0:T(8,128)(2,1)S(1)}, bf16[512,1280]{1,0:T(8,128)(2,1)}, u32[]{:S(2)}) copy-start(bf16[512,1280]{1,0:T(8,128)(2,1)} %param.22) | copy-start | bytes 3932164
  527.9 153.5 %copy-start.18 = (f32[1280]{0:T(1024)S(1)}, f32[1280]{0:T(1024)}, u32[]{:S(2)}) copy-start(f32[1280]{0:T(1024)} %copy-done.17) | copy-start | bytes 15364
  528.0 153.5 %copy-start.20 = (f32[512]{0:T(512)S(1)}, f32[512]{0:T(512)}, u32[]{:S(2)}) copy-start(f32[512]{0:T(512)} %copy-done.19) | copy-start | bytes 6148
  528.0 153.5 %copy-start.23 = (f32[512]{0:T(512)S(1)}, f32[512]{0:T(512)}, u32[]{:S(2)}) copy-start(f32[512]{0:T(512)} %copy-done.22) | copy-start | bytes 6148
  528.0 153.5 %copy-start.27 = (f32[1280]{0:T(1024)S(1)}, f32[1280]{0:T(1024)}, u32[]{:S(2)}) copy-start(f32[1280]{0:T(1024)} %copy-done.26) | copy-start | bytes 15364
  681.4 5.0 copy-start.13
  686.4 314.3 %reduce-scatter.11.cloned.1.call-start = ((), (), s32[]{:S(2)}) async-start(), calls=%async_computation.14 | async-start | bytes 6758400 | tf_op jit(solution)/shard_map/reduce_scatter | solution.py:278
  693.3 7.1 collective-permute-start.2
  694.6 8.0 collective-permute-start.3
  707.2 1.6 copy-start.9
  713.7 431.1 %reduce-scatter.9.cloned.1.call-start = ((), (), s32[]{:S(2)}) async-start(), calls=%async_computation.13 | async-start | bytes 6758400 | tf_op jit(solution)/shard_map/reduce_scatter | solution.py:277
  720.1 702.7 %reduce-scatter.15.cloned.1.call-start = ((), (), s32[]{:S(2)}) async-start(), calls=%async_computation.16 | async-start | bytes 27033600 | tf_op jit(solution)/shard_map/reduce_scatter | solution.py:284
  735.8 1.3 copy-start.12
  735.8 975.0 %reduce-scatter.17.cloned.1.call-start = ((), (), s32[]{:S(2)}) async-start(), calls=%async_computation.17 | async-start | bytes 27033600 | tf_op jit(solution)/shard_map/reduce_scatter | solution.py:286
  753.3 0.7 copy-start.28
  755.7 4.4 copy-start.4
  760.1 14.0 copy-start.10
  760.1 14.3 copy-start.29
  774.4 1.9 copy-start.30
  776.4 2.4 copy-start.25
  778.8 1.8 copy-start.6
  780.5 2.4 copy-start.21
Sparse Core Ops, SparseCore 0:
  10.9 62.3 all-gather.8
  76.2 57.8 all-gather.10
  136.9 77.5 all-gather.6
  217.3 57.6 all-gather.12
  277.7 97.2 all-gather.14
  377.7 96.6 all-gather.16
  519.2 143.5 reduce-scatter.12
  686.5 167.6 reduce-scatter.6
  857.1 143.5 reduce-scatter.10
  1003.4 141.3 reduce-scatter.8
  1147.8 274.9 reduce-scatter.14
  1425.5 285.2 reduce-scatter.16
where the time goes:
time: 1730 us; the launch traced here: 1720 us
  waiting for transfers between devices  1030 us (60%)
  matrix products  367 us (21%)
  blocking collectives  170 us (10%)
  other arithmetic  66.8 us (4%)
  local copies, waits for them, and re-layouts  53 us (3%)
    reduce_scatter x1, waiting for transfers between devices, body(): lax.psum_scatter(down_w_grad, 'dev', scatter_dimension=0, tiled=True)  288 us
    reduce_scatter x1, waiting for transfers between devices, body(): lax.psum_scatter(up_w_grad, 'dev', scatter_dimension=0, tiled=True)  278 us
    unnamed x2, blocking collectives  170 us
    reduce_scatter x1, waiting for transfers between devices, body(): lax.psum_scatter(key_w_grad, 'dev', scatter_dimension=0, tiled=True)  144 us
    dot_general x54, matrix products, dot_cols(): lax.dot_general(left, right, (((1,), (1,)), ((), ())), preferred_element_...  126 us
    dot_general x38, matrix products, matmul(): return jnp.dot(left, right, preferred_element_type=jnp.float32)  126 us
    dot_general x38, matrix products, dot_rows(): lax.dot_general(left, right, (((0,), (0,)), ((), ())), preferred_element_...  115 us
    reduce_scatter x1, waiting for transfers between devices, body(): lax.psum_scatter(value_w_grad, 'dev', scatter_dimension=0, tiled=True)  85.4 us
  transfers between devices with their start and end apart: 16, of which 11 were waited for; matrix products, arithmetic and copies ran while one was open for 25% of the time, Pallas kernels for 0%

commit v1 on v0

v1 whole, which is shorter than its diff:
```python
import functools
import math

import jax
import jax.numpy as jnp
from jax import lax
from jax.experimental import pallas as pl
from jax.experimental.pallas import tpu as pltpu
from jax.sharding import PartitionSpec as P

HD = 80
EPS = 1e-05
NEG = -1e30
SCALE = HD**-0.5
LOG2E = math.log2(math.e)
BF = jnp.bfloat16
F32 = jnp.float32
VECTORS = 128


def contract(left, right, left_dim, right_dim):
    return lax.dot_general(
        left, right, (((left_dim,), (right_dim,)), ((), ())), preferred_element_type=F32
    )


def attend_kernel(length, qkv, attended, log_total):
    rows = qkv.shape[2]
    keys = qkv[1].T
    dead = lax.broadcasted_iota(jnp.int32, (rows, 1), 0) >= length[0]
    scores = contract(keys, qkv[0], 1, 0) + jnp.where(dead, NEG, 0.0).astype(F32)
    top = jnp.max(scores, axis=0, keepdims=True)
    weights = jnp.exp2((scores - top) * (SCALE * LOG2E))
    total = jnp.sum(weights, axis=0, keepdims=True)
    probs = (weights * (1.0 / total)).astype(BF)
    attended[...] = contract(qkv[2], probs, 1, 0).astype(BF)
    log_total[0] = top * (SCALE * LOG2E) + jnp.log2(total)


def attend(length, qkv):
    _, width, rows = qkv.shape
    heads = width // HD
    return pl.pallas_call(
        attend_kernel,
        grid=(heads,),
        in_specs=[
            pl.BlockSpec(memory_space=pltpu.SMEM),
            pl.BlockSpec((3, HD, rows), lambda h: (0, h, 0)),
        ],
        out_specs=[
            pl.BlockSpec((HD, rows), lambda h: (h, 0)),
            pl.BlockSpec((1, 1, rows), lambda h: (h, 0, 0)),
        ],
        out_shape=[
            jax.ShapeDtypeStruct((width, rows), BF),
            jax.ShapeDtypeStruct((heads, 1, rows), F32),
        ],
        compiler_params=pltpu.CompilerParams(vmem_limit_bytes=40 << 20),
        cost_estimate=pl.CostEstimate(
            flops=12 * width * rows * rows,
            bytes_accessed=8 * width * rows,
            transcendentals=heads * rows * rows,
        ),
    )(length, qkv)


def attend_back_kernel(length, qkv, out_grad, log_total, grads, key_sum, value_sum, *, step):
    rows = qkv.shape[2]
    keys = qkv[1].T
    values = qkv[2].T
    dead = lax.broadcasted_iota(jnp.int32, (rows, 1), 0) >= length[0]
    bias = jnp.where(dead, NEG, 0.0).astype(F32)
    for at in range(0, rows, step):
        part = slice(at, at + step)
        queries = qkv[0, :, part]
        out_part = out_grad[:, part]
        scores = contract(keys, queries, 1, 0) + bias
        probs = jnp.exp2(scores * (SCALE * LOG2E) - log_total[0, :, part])
        prob_grad = contract(values, out_part, 1, 0)
        inner = jnp.sum(probs * prob_grad, axis=0, keepdims=True)
        score_grad = (probs * (prob_grad - inner)).astype(BF)
        probs_low = probs.astype(BF)
        grads[0, :, part] = (contract(qkv[1], score_grad, 1, 0) * SCALE).astype(BF)
        key_part = contract(queries, score_grad, 1, 1)
        value_part = contract(out_part, probs_low, 1, 1)
        if at == 0:
            key_sum[...] = key_part
            value_sum[...] = value_part
        else:
            key_sum[...] += key_part
            value_sum[...] += value_part
    grads[1] = (key_sum[...] * SCALE).astype(BF)
    grads[2] = value_sum[...].astype(BF)


def attend_back(length, qkv, out_grad, log_total):
    _, width, rows = qkv.shape
    heads = width // HD
    return pl.pallas_call(
        functools.partial(attend_back_kernel, step=min(512, rows)),
        grid=(heads,),
        in_specs=[
            pl.BlockSpec(memory_space=pltpu.SMEM),
            pl.BlockSpec((3, HD, rows), lambda h: (0, h, 0)),
            pl.BlockSpec((HD, rows), lambda h: (h, 0)),
            pl.BlockSpec((1, 1, rows), lambda h: (h, 0, 0)),
        ],
        out_specs=pl.BlockSpec((3, HD, rows), lambda h: (0, h, 0)),
        out_shape=jax.ShapeDtypeStruct((3, width, rows), BF),
        scratch_shapes=[pltpu.VMEM((HD, rows), F32), pltpu.VMEM((HD, rows), F32)],
        compiler_params=pltpu.CompilerParams(vmem_limit_bytes=48 << 20),
        cost_estimate=pl.CostEstimate(
            flops=22 * width * rows * rows,
            bytes_accessed=14 * width * rows,
            transcendentals=heads * rows * rows,
        ),
    )(length, qkv, out_grad, log_total)


def make_body(devices):
    chips = devices // 2
    lines = chips // 4

    def place(line, b, a, core):
        return ((line * 2 + b) * 2 + a) * 2 + core

    every = [
        (line, b, a, core)
        for line in range(lines)
        for b in range(2)
        for a in range(2)
        for core in range(2)
    ]
    core_pairs = [(place(*at), place(at[0], at[1], at[2], 1 - at[3])) for at in every]
    a_pairs = [(place(*at), place(at[0], at[1], 1 - at[2], at[3])) for at in every]
    b_pairs = [(place(*at), place(at[0], 1 - at[1], at[2], at[3])) for at in every]
    groups = [
        [place(line, b, a, core) for line in range(lines)]
        for b in range(2)
        for a in range(2)
        for core in range(2)
    ]
    half = lines // 2

    def swap_core(value):
        return lax.ppermute(value, "dev", core_pairs)

    def swap_a(value):
        return lax.ppermute(value, "dev", a_pairs)

    def swap_b(value):
        return lax.ppermute(value, "dev", b_pairs)

    def body(
        tokens,
        lengths,
        out_grad,
        first_gain,
        first_shift,
        query_weight,
        query_bias,
        key_weight,
        value_weight,
        value_bias,
        proj_weight,
        proj_bias,
        mid_gain,
        mid_shift,
        up_weight,
        up_bias,
        down_weight,
        down_bias,
    ):
        position = lax.axis_index("dev")
        core = position % 2
        chip = position // 2
        at_a = chip % 2
        at_b = (chip // 2) % 2
        own_rows, width = tokens.shape
        rows = 2 * own_rows
        shard = query_weight.shape[0]
        side = width // 2
        hidden = up_weight.shape[1]
        block = hidden // devices
        spread = block // shard
        length = lax.dynamic_slice(lengths, (chip,), (1,))

        def both(own, other):
            first = jnp.where(core == 0, own, other)
            second = jnp.where(core == 0, other, own)
            return jnp.concatenate([first, second], axis=0)

        def columns(weight, which):
            return lax.dynamic_slice(weight, (0, which * side), (weight.shape[0], side))

        def blocks(weight, which):
            cut = weight.reshape(weight.shape[0], chips, 2, block)
            return lax.dynamic_index_in_dim(cut, which, 2, keepdims=False).reshape(
                weight.shape[0], chips * block
            )

        def gather(value):
            line = lax.all_gather(value, "dev", axis=0, axis_index_groups=groups)
            from_a = swap_a(line)
            from_b = swap_b(line)
            far_low = swap_a(from_b[:half])
            far_high = swap_b(from_a[half:])
            whole = jnp.zeros((lines, 2, 2) + value.shape, value.dtype)
            zero = jnp.int32(0)

            def put(whole, part, line_at, b, a):
                return lax.dynamic_update_slice(
                    whole, part[:, None, None], (jnp.int32(line_at), b, a, zero, zero)
                )

            whole = put(whole, line, 0, at_b, at_a)
            whole = put(whole, from_a, 0, at_b, 1 - at_a)
            whole = put(whole, from_b, 0, 1 - at_b, at_a)
            whole = put(whole, far_low, 0, 1 - at_b, 1 - at_a)
            whole = put(whole, far_high, half, 1 - at_b, 1 - at_a)
            return whole.reshape(chips * value.shape[0], value.shape[1])

        def scatter_plane(whole):
            parts = whole.reshape(lines, 2, 2, whole.shape[0] // chips, whole.shape[1])

            def pick(b, a):
                at = lax.dynamic_index_in_dim(parts, b, 1, keepdims=False)
                return lax.dynamic_index_in_dim(at, a, 1, keepdims=False)

            far = pick(1 - at_b, 1 - at_a).astype(BF)
            far_low = swap_a(far[:half])
            far_high = swap_b(far[half:])
            to_a = pick(at_b, 1 - at_a).astype(F32)
            to_b = pick(1 - at_b, at_a).astype(F32)
            to_a = jnp.concatenate([to_a[:half], to_a[half:] + far_high.astype(F32)], axis=0)
            to_b = jnp.concatenate([to_b[:half] + far_low.astype(F32), to_b[half:]], axis=0)
            from_a = swap_a(to_a.astype(BF))
            from_b = swap_b(to_b.astype(BF))
            own = pick(at_b, at_a).astype(F32) + from_a.astype(F32) + from_b.astype(F32)
            return own.astype(BF)

        def scatter_line(parts):
            return lax.psum_scatter(
                parts, "dev", scatter_dimension=0, axis_index_groups=groups
            )

        other = 1 - core
        vectors = jnp.stack(
            [first_gain, first_shift, query_bias, value_bias, proj_bias, mid_gain, mid_shift, down_bias],
            axis=1,
        )
        vectors = jnp.concatenate([vectors, up_bias.reshape(shard, spread)], axis=1)
        vectors = jnp.pad(vectors, ((0, 0), (0, VECTORS - vectors.shape[1])))
        own_qkv = jnp.concatenate(
            [columns(query_weight, core), columns(key_weight, core), columns(value_weight, core), vectors], axis=1
        )
        give_qkv = jnp.concatenate(
            [columns(query_weight, other), columns(key_weight, other), columns(value_weight, other), vectors], axis=1
        )
        qkv_shard = both(own_qkv, swap_core(give_qkv))
        all_tokens = both(tokens, swap_core(tokens)).astype(F32)
        rest_own = jnp.concatenate([columns(proj_weight, core), blocks(up_weight, core)], axis=1)
        rest_give = jnp.concatenate([columns(proj_weight, other), blocks(up_weight, other)], axis=1)
        rest_shard = both(rest_own, swap_core(rest_give))
        all_grad = both(out_grad, swap_core(out_grad))
        live = jnp.arange(rows) < length[0]
        grad_low = jnp.where(live[:, None], all_grad, jnp.zeros_like(all_grad))

        w_qkv_wide = gather(qkv_shard)
        w_proj_side = gather(rest_shard[:, :side])
        w_up = gather(rest_shard[:, side:])
        w_down = gather(down_weight)

        w_qkv = w_qkv_wide[:, : 3 * side]
        table = w_qkv_wide[:, 3 * side :].astype(F32).T
        gain_one, shift_one, b_query, b_value, b_proj, gain_two, shift_two, b_down = (
            table[i] for i in range(8)
        )
        hidden_bias = table[8 : 8 + spread].reshape(spread, chips, 2, shard)
        hidden_bias = lax.dynamic_index_in_dim(hidden_bias, core, 2, keepdims=False)
        hidden_bias = hidden_bias.transpose(1, 2, 0).reshape(chips * block)
        w_proj_other = swap_core(w_proj_side)
        w_proj = jnp.concatenate(
            [
                jnp.where(core == 0, w_proj_side, w_proj_other),
                jnp.where(core == 0, w_proj_other, w_proj_side),
            ],
            axis=1,
        )

        def own_side(vector):
            return lax.dynamic_slice(vector, (core * side,), (side,))

        def normalize(value, gain, shift):
            center = value - jnp.mean(value, axis=-1, keepdims=True)
            spread_of = jnp.mean(center * center, axis=-1, keepdims=True)
            scale = lax.rsqrt(spread_of + EPS)
            hat = center * scale
            return hat * gain + shift, hat, scale

        def normalize_back(grad, hat, scale, gain):
            scaled = grad * gain
            mean = jnp.mean(scaled, axis=-1, keepdims=True)
            dot = jnp.mean(scaled * hat, axis=-1, keepdims=True)
            return (
                (scaled - mean - hat * dot) * scale,
                jnp.sum(grad * hat, axis=0),
                jnp.sum(grad, axis=0),
            )

        normed = normalize(all_tokens, gain_one, shift_one)[0].astype(BF)
        qkv_bias = jnp.concatenate([own_side(b_query), jnp.zeros((side,), F32), own_side(b_value)])
        qkv = (contract(w_qkv, normed, 0, 1) + qkv_bias[:, None]).astype(BF).reshape(3, side, rows)
        attended_own, log_total = attend(length, qkv)
        attended = both(attended_own, swap_core(attended_own))
        mid = all_tokens + contract(attended, w_proj, 0, 0) + b_proj
        mid_normed, mid_hat, mid_scale = normalize(mid, gain_two, shift_two)
        mid_low = mid_normed.astype(BF)
        pre_act = contract(mid_low, w_up, 1, 0) + hidden_bias
        below = 0.5 + 0.5 * lax.erf(pre_act * math.sqrt(0.5))
        activ = (pre_act * below).astype(BF)
        slope = (below + pre_act * (jnp.exp(-0.5 * pre_act * pre_act) * (1.0 / math.sqrt(2.0 * math.pi)))).astype(BF)
        down_grad = contract(activ, grad_low, 0, 0).astype(BF)
        down_part = contract(activ, w_down, 1, 0)

        def rows_of(value, which):
            return lax.dynamic_slice(value, (which * own_rows, 0), (own_rows, value.shape[1]))

        down_other = swap_core(rows_of(down_part, other).astype(BF))
        output = (
            rows_of(mid, core) + rows_of(down_part, core) + down_other.astype(F32) + b_down
        ).astype(BF)

        grad_full = grad_low.astype(F32)
        down_b_grad = 0.5 * jnp.sum(grad_full, axis=0)
        pre_grad = (contract(grad_low, w_down, 1, 1) * slope.astype(F32)).astype(BF)
        up_grad = contract(mid_low, pre_grad, 0, 0).astype(BF)
        up_b_grad = jnp.sum(pre_grad.astype(F32), axis=0)
        mid_part = contract(pre_grad, w_up, 1, 1)
        mid_e = mid_part + swap_core(mid_part.astype(BF)).astype(F32)
        mid_back, gain_two_grad, shift_two_grad = normalize_back(mid_e, mid_hat, mid_scale, gain_two)
        mid_grad = grad_full + mid_back
        branch = mid_grad.astype(BF)
        branch_side = lax.dynamic_slice(branch, (0, core * side), (rows, side))
        proj_grad = contract(attended, branch_side, 1, 0).astype(BF)
        proj_b_grad = 0.5 * jnp.sum(branch.astype(F32), axis=0)
        w_proj_heads = lax.dynamic_slice(w_proj, (core * side, 0), (side, width))
        attended_grad = contract(w_proj_heads, branch, 1, 1).astype(BF)
        qkv_back = attend_back(length, qkv, attended_grad, log_total).reshape(3 * side, rows)
        qkv_grad = contract(normed, qkv_back, 0, 1).astype(BF)
        qkv_b_grad = jnp.sum(qkv_back.astype(F32), axis=1)
        normed_part = contract(qkv_back, w_qkv, 0, 1)
        normed_other = swap_core(rows_of(normed_part, other).astype(BF))
        normed_e = rows_of(normed_part, core) + normed_other.astype(F32)
        _, first_hat, first_scale = normalize(tokens.astype(F32), gain_one, shift_one)
        first_back, gain_one_grad, shift_one_grad = normalize_back(normed_e, first_hat, first_scale, gain_one)
        input_grad = (rows_of(mid_grad, core) + first_back).astype(BF)

        def on_side(vector):
            return lax.dynamic_update_slice(jnp.zeros((width,), F32), vector, (core * side,))

        up_rows = up_b_grad.reshape(chips, 1, shard, spread)
        up_rows = lax.dynamic_update_slice(
            jnp.zeros((chips, 2, shard, spread), F32), up_rows, (0, core, 0, 0)
        ).reshape(width, spread)
        sums = jnp.stack(
            [
                gain_one_grad,
                shift_one_grad,
                on_side(qkv_b_grad[:side]),
                on_side(qkv_b_grad[2 * side :]),
                proj_b_grad,
                0.5 * gain_two_grad,
                0.5 * shift_two_grad,
                down_b_grad,
            ],
            axis=1,
        )
        sums = jnp.concatenate([sums, up_rows], axis=1)
        sums = jnp.pad(sums, ((0, 0), (0, VECTORS - sums.shape[1])))

        down_sum = scatter_line(scatter_plane(down_grad))
        up_sum = scatter_line(scatter_plane(up_grad))
        proj_sum = scatter_line(scatter_plane(proj_grad))
        qkv_sum = scatter_line(scatter_plane(qkv_grad))
        vector_sum = scatter_line(scatter_plane(sums))

        def finish(sum_of, which):
            return lax.dynamic_slice(sum_of, (which * shard, 0), (shard, sum_of.shape[1]))

        tail = jnp.concatenate([proj_sum, qkv_sum, vector_sum, up_sum], axis=1)
        mine = finish(tail, core)
        theirs = swap_core(finish(tail, other))
        left = jnp.where(core == 0, mine, theirs).astype(F32)
        right = jnp.where(core == 0, theirs, mine).astype(F32)

        def joined(start):
            return jnp.concatenate([left[:, start : start + side], right[:, start : start + side]], axis=1)

        at_vectors = 4 * side
        vector_rows = (
            left[:, at_vectors : at_vectors + 8 + spread] + right[:, at_vectors : at_vectors + 8 + spread]
        )
        at_up = at_vectors + VECTORS
        up_all = jnp.stack(
            [
                left[:, at_up:].reshape(shard, chips, block),
                right[:, at_up:].reshape(shard, chips, block),
            ],
            axis=2,
        ).reshape(shard, hidden)
        return (
            output,
            input_grad,
            vector_rows[:, 0],
            vector_rows[:, 1],
            joined(side),
            vector_rows[:, 2],
            joined(2 * side),
            joined(3 * side),
            vector_rows[:, 3],
            joined(0),
            vector_rows[:, 4],
            vector_rows[:, 5],
            vector_rows[:, 6],
            up_all,
            vector_rows[:, 8 : 8 + spread].reshape(block),
            down_sum.astype(F32),
            vector_rows[:, 7],
        )

    return body


def solution(mesh):
    matrix, vector = P("dev", None), P("dev")
    return jax.shard_map(
        make_body(mesh.shape["dev"]),
        mesh=mesh,
        in_specs=(
            matrix,
            P(),
            matrix,
            vector,
            vector,
            matrix,
            vector,
            matrix,
            matrix,
            vector,
            matrix,
            vector,
            vector,
            vector,
            matrix,
            vector,
            matrix,
            vector,
        ),
        out_specs=(
            matrix,
            matrix,
            vector,
            vector,
            matrix,
            vector,
            matrix,
            matrix,
            vector,
            matrix,
            vector,
            vector,
            vector,
            matrix,
            vector,
            matrix,
            vector,
        ),
        check_vma=False,
    )
```

time: 1730 us -> 600 us (0.35)
  waiting for transfers between devices: 1030 us -> 202 us
  matrix products: 367 us -> 103 us
  blocking collectives: 170 us -> 21.4 us
  Pallas kernels: 0 us -> 47.5 us
  local copies, waits for them, and re-layouts: 53 us -> 91.3 us
  starting transfers between devices: 11.4 us -> 41.6 us
    reduce_scatter x6 -> x5, waiting for transfers between devices: 795 us -> 24.8 us  [scatter_line(): lax.psum_scatter(parts, 'dev', scatter_dimension=0, axis_index_groups=gro...]
    dot_general x130 -> x12, matrix products: 367 us -> 103 us  [contract(): lax.dot_general(left, right, (((left_dim,), (right_dim,)), ((), ())), pre...]
    all_gather x6 -> x3, waiting for transfers between devices: 231 us -> 46.7 us  [gather(): line = lax.all_gather(value, 'dev', axis=0, axis_index_groups=groups)]
    unnamed x2 -> x0, blocking collectives: 170 us -> none
    ppermute x4 -> x46, waiting for transfers between devices: 3.54 us -> 129 us  [the longest x18 76.8 us: swap_b(): return lax.ppermute(value, 'dev', b_pairs)]
    pallas_call x0 -> x2, Pallas kernels: none -> 47.5 us  [the longest x1 31.7 us: attend_back(): pl.pallas_call(functools.partial(attend_back_kernel, step=min(512, rows))...]
    dynamic_update_slice x16 -> x23, local copies, waits for them, and re-layouts: 0.97 us -> 32.6 us  [the longest x20 31.7 us: put(): lax.dynamic_update_slice(whole, part[:, None, None], (jnp.int32(line_at),...]
    ppermute x4 -> x46, starting transfers between devices: 10.7 us -> 41 us  [the longest x18 21 us: swap_b(): return lax.ppermute(value, 'dev', b_pairs)]
  transfers between devices with their start and end apart: 16 -> 54, of which waited for: 11 -> 26; matrix products, arithmetic and copies ran while one was open for 25% -> 31% of each run, Pallas kernels for 0% -> 8%
where the time goes in v1:
time: 600 us; the launch traced here: 593 us
  waiting for transfers between devices  202 us (34%)
  matrix products  103 us (17%)
  local copies, waits for them, and re-layouts  91.3 us (15%)
  other arithmetic  70.1 us (12%)
  Pallas kernels  47.5 us (8%)
  starting transfers between devices  41.6 us (7%)
  blocking collectives  21.4 us (4%)
  between operations  15.8 us (3%)
    dot_general x12, matrix products, contract(): lax.dot_general(left, right, (((left_dim,), (right_dim,)), ((), ())), pre...  103 us
    ppermute x18, waiting for transfers between devices, swap_b(): return lax.ppermute(value, 'dev', b_pairs)  76.8 us
    ppermute x18, waiting for transfers between devices, swap_a(): return lax.ppermute(value, 'dev', a_pairs)  51.6 us
    all_gather x3, waiting for transfers between devices, gather(): line = lax.all_gather(value, 'dev', axis=0, axis_index_groups=groups)  46.7 us
    dynamic_update_slice x20, local copies, waits for them, and re-layouts, put(): lax.dynamic_update_slice(whole, part[:, None, None], (jnp.int32(line_at),...  31.7 us
    pallas_call x1, Pallas kernels, attend_back(): pl.pallas_call(functools.partial(attend_back_kernel, step=min(512, rows))...  31.7 us
    reduce_scatter x5, waiting for transfers between devices, scatter_line(): lax.psum_scatter(parts, 'dev', scatter_dimension=0, axis_index_groups=gro...  24.8 us
    all_gather x1, blocking collectives, gather(): line = lax.all_gather(value, 'dev', axis=0, axis_index_groups=groups)  21.4 us
  transfers between devices with their start and end apart: 54, of which 26 were waited for; matrix products, arithmetic and copies ran while one was open for 31% of the time, Pallas kernels for 8%

profile of v1, /device:TPU:0, one launch (start us, length us, event | category | flops | bytes accessed | tf_op | source)
XLA Modules:
  0.0 592.7 jit_solution(7474441991174144724)
XLA Ops:
  15.7 4.1 dynamic-slice_reduce_fusion.1
  23.0 21.4 %all-gather.1 = bf16[320,640]{1,0:T(8,128)(2,1)S(1)} all-gather(bf16[80,640]{1,0:T(8,128)(2,1)S(1)} %pad_maximum_fusion.24), channel_id=3, replica_groups={{0,8,16,24},{1,9,17,25},{2,10,18,26},{3,11,19,27},{4,12,20,28},{5,13,21..., dimensions={0}, use_global_device_ids=true | all-gather | bytes 512000 | tf_op jit(solution)/shard_map/all_gather | solution.py:203
  50.6 3.5 collective-permute-done.8
  58.9 3.3 collective-permute-done.10
  66.9 3.0 broadcast_select_fusion.5
  71.5 3.0 broadcast_in_dim.101
  75.7 19.1 %all-gather.12.cloned.1.call-done = bf16[640,1280]{1,0:T(8,128)(2,1)} async-done(((bf16[160,1280]{1,0:T(8,128)(2,1)}), bf16[640,1280]{1,0:T(8,128)(2,1)}) %all-gather.12.cloned.1.call-update) | async-done | bytes 1638416 | tf_op jit(solution)/shard_map/all_gather | solution.py:203
  97.8 3.4 broadcast_in_dim.120
  102.5 4.0 broadcast_select_fusion.1
  106.5 27.5 %all-gather.10.cloned.1.call-done = bf16[320,2560]{1,0:T(8,128)(2,1)} async-done(((bf16[80,2560]{1,0:T(8,128)(2,1)}), bf16[320,2560]{1,0:T(8,128)(2,1)}) %all-gather.10.cloned.1.call-update) | async-done | bytes 1638416 | tf_op jit(solution)/shard_map/all_gather | solution.py:203
  139.4 1.6 slice.469
  142.7 2.5 bitcast_dynamic-update-slice_fusion.5
  145.3 2.5 bitcast_dynamic-update-slice_fusion.4
  148.4 2.7 bitcast_dynamic-update-slice_fusion.1
  151.1 2.1 slice.485
  154.6 2.7 bitcast_dynamic-update-slice_fusion
  157.3 2.1 slice.484
  159.4 26.4 %collective-permute-done.4 = bf16[2,80,2048]{2,1,0:T(8,128)(2,1)S(1)} collective-permute-done((bf16[2,80,2048]{2,1,0:T(8,128)(2,1)S(1)}, bf16[2,80,2048]{2,1,0:T(8,128)(2,1)S(1)}, u32[]{:S(2)}, u32[]{:S(2)}) %collective-permute-start.4) | collective-permute-done | bytes 655392 | tf_op jit(solution)/shard_map/ppermute | solution.py:149
  188.2 2.7 collective-permute-done.5
  192.8 2.9 fusion.75
  196.0 11.0 %add_convert_fusion = bf16[1920,1024]{1,0:T(8,128)(2,1)} fusion(f32[1920]{0:T(1024)S(1)} %pad_maximum_fusion.27, bf16[1280,2048]{1,0:T(8,128)(2,1)} %bitcast.17, f32[1280]{0:T(1024)S(1)} %get-tuple-element.97, f32[1280]{0:T(1024)S(1)} %get-tuple-element.96, f32[1024]{0:T(1024)S(1)} %add_rsqrt_fusion.1, f32[1024]{0:T(1024)S(1)} %broadcast_multiply_fusion.7, ...), kind=kOutput, calls=%fused_computation.13 | convolution fusion | flops 5048893440 | bytes 11494912 | tf_op jit(solution)/shard_map/dot_general | solution.py:22
  207.5 2.1 copy-done.1
  209.6 15.9 %shard_map.305 = (bf16[640,1024]{1,0:T(8,128)(2,1)S(1)}, f32[8,1,1024]{2,1,0:T(1,128)S(1)}) custom-call(s32[1]{0:T(128)} %dynamic_slice.168.length, bf16[3,640,1024]{2,1,0:T(8,128)(2,1)S(1)} %bitcast.312), custom_call_target="tpu_custom_call" | custom-call | flops 8053063680 | bytes 5242880 | tf_op jit(solution)/shard_map/pallas_call | solution.py:43
  230.2 2.7 bitcast_dynamic-update-slice_fusion.3
  232.9 2.7 bitcast_dynamic-update-slice_fusion.2
  235.6 2.1 bitcast_dynamic-update-slice_fusion.6
  237.7 2.1 bitcast_dynamic-update-slice_fusion.8
  239.8 10.2 %collective-permute-done.15 = bf16[2,80,2560]{2,1,0:T(8,128)(2,1)S(1)} collective-permute-done((bf16[2,80,2560]{2,1,0:T(8,128)(2,1)S(1)}, bf16[2,80,2560]{2,1,0:T(8,128)(2,1)S(1)}, u32[]{:S(2)}, u32[]{:S(2)}) %collective-permute-start.15) | collective-permute-done | bytes 819232 | tf_op jit(solution)/shard_map/ppermute | solution.py:149
  255.1 4.3 fusion.76
  260.2 10.7 %multiply_convert_fusion.1 = (bf16[1024,2560]{1,0:T(8,128)(2,1)}, f32[1024,2560]{1,0:T(8,128)}) fusion(f32[2560]{0:T(1024)S(1)} %add.476, bf16[1280,2560]{1,0:T(8,128)(2,1)S(1)} %bitcast.325, f32[1024,1280]{1,0:T(8,128)S(1)} %get-tuple-element.117, f32[1280]{0:T(1024)S(1)} %get-tuple-element.100, f32[1280]{0:T(1024)S(1)} %get-tuple-element.99, ...), kind=kOutput, calls=%fused_computation.10 | convolution fusion | flops 6733168640 | bytes 27553792 | tf_op jit(solution)/shard_map/dot_general | solution.py:22
  270.9 15.3 %convert_reduce_fusion = (f32[2560]{0:T(1024)S(1)}, bf16[1024,2560]{1,0:T(8,128)(2,1)}) fusion(f32[1024,2560]{1,0:T(8,128)} %get-tuple-element.119, f32[2560]{0:T(1024)S(1)} %add.476, bf16[2560,1280]{1,0:T(8,128)(2,1)} %bitcast.54, bf16[512,1280]{1,0:T(8,128)(2,1)S(1)} %copy-done.14, bf16[512,1280]{1,0:T(8,128)(2,1)S(1)} %copy-done.11, ...), kind=kOutput, calls=%fused_computation.8 | convolution fusion | flops 6756759040 | bytes 24925184 | tf_op jit(solution)/shard_map/dot_general | solution.py:22
  286.2 11.4 %fusion.77 = (bf16[1024,1280]{1,0:T(8,128)(2,1)}, f32[1024,1280]{1,0:T(8,128)}) fusion(bf16[1024,2560]{1,0:T(8,128)(2,1)} %get-tuple-element.123, bf16[1280,2560]{1,0:T(8,128)(2,1)S(1)} %bitcast.326), kind=kOutput, calls=%fused_computation.260 | convolution fusion | flops 6712197120 | bytes 19660800 | tf_op jit(solution)/shard_map/dot_general | solution.py:22
  297.7 8.0 %convolution_convert_fusion.1 = bf16[1280,2560]{1,0:T(8,128)(2,1)S(1)} fusion(bf16[1024,2560]{1,0:T(8,128)(2,1)S(1)} %copy-done.54, f32[1024,1280]{1,0:T(8,128)S(1)} %get-tuple-element.117, f32[1280]{0:T(1024)S(1)} %get-tuple-element.100, f32[1280]{0:T(1024)S(1)} %get-tuple-element.99, f32[1024]{0:T(1024)S(1)} %add_rsqrt_fusion, ...), kind=kOutput, calls=%fused_computation.2 | convolution fusion | flops 6720716800 | bytes 17057792 | tf_op jit(solution)/shard_map/dot_general | solution.py:22
  305.7 1.6 dynamic-slice_bitcast_fusion.11
  307.4 1.7 copy-done.8
  312.6 1.8 copy.142
  316.1 12.9 %collective-permute-done.37 = bf16[2,80,2560]{2,1,0:T(8,128)(2,1)} collective-permute-done((bf16[2,80,2560]{2,1,0:T(8,128)(2,1)}, bf16[2,80,2560]{2,1,0:T(8,128)(2,1)}, u32[]{:S(2)}, u32[]{:S(2)}) %collective-permute-start.37) | collective-permute-done | bytes 819232 | tf_op jit(solution)/shard_map/ppermute | solution.py:152
  329.2 2.3 fusion.42
  336.3 6.8 %multiply_reduce_fusion = (f32[1280]{0:T(1024)S(1)}, f32[1024]{0:T(1024)S(1)}, f32[1024]{0:T(1024)S(1)}, f32[1280]{0:T(1024)S(1)}) fusion(f32[1024,1280]{1,0:T(8,128)} %copy-done.2, f32[1024]{0:T(1024)S(1)} %copy-done.40, f32[1024]{0:T(1024)S(1)} %copy-done.38, f32[1024,1280]{1,0:T(8,128)} %get-tuple-element.121, ...), kind=kLoop, calls=%fused_computation.27 | loop fusion | flops 14413312 | bytes 13138944 | tf_op jit(solution)/shard_map/reduce_sum | solution.py:307
  343.7 6.9 %convert_reduce_fusion.4 = (f32[1280]{0:T(1024)S(1)}, bf16[1024,1280]{1,0:T(8,128)(2,1)S(1)}, f32[1024,1280]{1,0:T(8,128)}, f32[1280]{0:T(1024)S(1)}) fusion(f32[1024]{0:T(1024)S(1)} %broadcast_multiply_fusion.4, f32[1024]{0:T(1024)S(1)} %copy-done.40, f32[1024,1280]{1,0:T(8,128)S(1)} %bitcast.314, f32[1024]{0:T(1024)S(1)} %copy-done.38, ...), kind=kLoop, calls=%fused_computation.28 | loop fusion | flops 26211840 | bytes 23625728 | tf_op jit(solution)/shard_map/reduce_sum | solution.py:346
  350.6 1.9 fusion.43.out_grad
  352.5 2.2 convolution_convert_fusion.3
  354.8 31.7 %shard_map.306 = bf16[3,640,1024]{2,1,0:T(8,128)(2,1)S(1)} custom-call(s32[1]{0:T(128)} %dynamic_slice.168.length, bf16[3,640,1024]{2,1,0:T(8,128)(2,1)} %bitcast.311, bf16[640,1024]{1,0:T(8,128)(2,1)S(1)} %fusion.43.out_grad, f32[8,1,1024]{2,1,0:T(1,128)S(1)} %get-tuple-element.20.log_total), custom_call_target="tpu_custom_call" | custom-call | flops 14763950080 | bytes 9175040 | tf_op jit(solution)/shard_map/pallas_call | solution.py:99
  387.1 8.8 %fusion.12 = f32[1024,1280]{1,0:T(8,128)S(1)} fusion(bf16[1920,1024]{1,0:T(8,128)(2,1)S(1)} %bitcast.309, bf16[1280,2048]{1,0:T(8,128)(2,1)} %bitcast.17), kind=kOutput, calls=%fused_computation.35 | convolution fusion | flops 5033164800 | bytes 14090240 | tf_op jit(solution)/shard_map/dot_general | solution.py:22
  399.2 2.7 collective-permute-done.25
  405.7 5.7 collective-permute-done.28
  413.7 4.6 fusion.32
  420.4 2.5 collective-permute-done.33
  425.0 2.4 collective-permute-done.34
  429.2 4.2 fusion.21
  433.5 9.5 %convolution_convert_fusion.2 = bf16[1280,1920]{1,0:T(8,128)(2,1)S(1)} fusion(bf16[1920,1024]{1,0:T(8,128)(2,1)} %bitcast.310, f32[1280]{0:T(1024)S(1)} %copy-done.48, f32[1280]{0:T(1024)S(1)} %get-tuple-element.96, f32[1024]{0:T(1024)S(1)} %copy-done.50, f32[1024]{0:T(1024)S(1)} %copy-done.46, bf16[512,1280]{1,0:T(8,128)(2,1)} %copy-done.4, ...), kind=kOutput, calls=%fused_computation.17 | convolution fusion | flops 5047418880 | bytes 11487232 | tf_op jit(solution)/shard_map/dot_general | solution.py:22
  445.2 9.2 %convolution_convert_fusion = bf16[2560,1280]{1,0:T(8,128)(2,1)S(1)} fusion(bf16[1024,2560]{1,0:T(8,128)(2,1)} %get-tuple-element.118, bf16[512,1280]{1,0:T(8,128)(2,1)S(1)} %copy-done.16, bf16[512,1280]{1,0:T(8,128)(2,1)S(1)} %copy-done.13, pred[1024]{0:T(1024)(128)(4,1)S(1)} %copy-done.52), kind=kOutput, calls=%fused_computation.1 | convolution fusion | flops 6720716800 | bytes 14418944 | tf_op jit(solution)/shard_map/dot_general | solution.py:22
  457.6 1.6 collective-permute-start.32
  460.0 16.0 %collective-permute-done.42 = bf16[2,160,1280]{2,1,0:T(8,128)(2,1)S(1)} collective-permute-done((bf16[2,160,1280]{2,1,0:T(8,128)(2,1)S(1)}, bf16[2,160,1280]{2,1,0:T(8,128)(2,1)S(1)}, u32[]{:S(2)}, u32[]{:S(2)}) %collective-permute-start.42) | collective-permute-done | bytes 819232 | tf_op jit(solution)/shard_map/ppermute | solution.py:152
  482.3 20.0 %collective-permute-done.32 = bf16[4,80,1920]{2,1,0:T(8,128)(2,1)S(1)} collective-permute-done((bf16[4,80,1920]{2,1,0:T(8,128)(2,1)S(1)}, bf16[4,80,1920]{2,1,0:T(8,128)(2,1)S(1)}, u32[]{:S(2)}, u32[]{:S(2)}) %collective-permute-start.32) | collective-permute-done | bytes 1228832 | tf_op jit(solution)/shard_map/ppermute | solution.py:152
  505.2 11.0 %fusion.78 = f32[1024,1280]{1,0:T(8,128)S(1)} fusion(bf16[1024,2560]{1,0:T(8,128)(2,1)} %get-tuple-element.118, bf16[2560,1280]{1,0:T(8,128)(2,1)} %bitcast.54), kind=kOutput, calls=%fused_computation.261 | convolution fusion | flops 6710886400 | bytes 17039360 | tf_op jit(solution)/shard_map/dot_general | solution.py:22
  516.2 2.4 copy-done.18
  519.8 12.7 %collective-permute-done.45 = bf16[4,160,1280]{2,1,0:T(8,128)(2,1)S(1)} collective-permute-done((bf16[4,160,1280]{2,1,0:T(8,128)(2,1)}, bf16[4,160,1280]{2,1,0:T(8,128)(2,1)S(1)}, u32[]{:S(2)}, u32[]{:S(2)}) %collective-permute-start.45) | collective-permute-done | bytes 1638432 | tf_op jit(solution)/shard_map/ppermute | solution.py:152
  533.6 3.7 fusion.19
  537.3 4.6 add_convert_fusion.2
  541.9 3.8 fusion.31
  547.0 24.8 %reduce-scatter.14.cloned.1.call-done = bf16[1,160,1280]{2,1,0:T(8,128)(2,1)} async-done(((bf16[4,160,1280]{2,1,0:T(8,128)(2,1)}), bf16[1,160,1280]{2,1,0:T(8,128)(2,1)}) %reduce-scatter.14.cloned.1.call-update) | async-done | bytes 409616 | tf_op jit(solution)/shard_map/reduce_scatter | solution.py:243
  571.8 1.9 bitcast_convert_fusion
  580.2 2.7 reshape.326
  (352 shorter events, 113.5 us)
Async XLA Ops:
  7.2 62.8 %all-gather.8.cloned.1.call-start = ((), (), s32[]{:S(2)}) async-start(), calls=%async_computation.10 | async-start | bytes 1638400 | tf_op jit(solution)/shard_map/all_gather | solution.py:203
  11.7 1.5 collective-permute-start.1
  14.1 80.8 %all-gather.12.cloned.1.call-start = ((), (), s32[]{:S(2)}) async-start(), calls=%async_computation.12 | async-start | bytes 2048000 | tf_op jit(solution)/shard_map/all_gather | solution.py:203
  14.8 119.3 %all-gather.10.cloned.1.call-start = ((), (), s32[]{:S(2)}) async-start(), calls=%async_computation.11 | async-start | bytes 2048000 | tf_op jit(solution)/shard_map/all_gather | solution.py:203
  20.2 2.7 collective-permute-start.7
  20.7 45.8 %collective-permute-start.22 = (bf16[512,1280]{1,0:T(8,128)(2,1)}, bf16[512,1280]{1,0:T(8,128)(2,1)}, u32[]{:S(2)}, u32[]{:S(2)}) collective-permute-start(bf16[512,1280]{1,0:T(8,128)(2,1)} %param.20), channel_id=1, source_target_pairs={{0,1},{1,0},{2,3},{3,2},{4,5},{5,4},{6,7},{7,6},{8,9},{9,8},{10,11... | collective-permute-start | bytes 3932168 | tf_op jit(solution)/shard_map/ppermute | solution.py:146
  20.8 42.8 %collective-permute-start = (bf16[512,1280]{1,0:T(8,128)(2,1)S(1)}, bf16[512,1280]{1,0:T(8,128)(2,1)}, u32[]{:S(2)}, u32[]{:S(2)}) collective-permute-start(bf16[512,1280]{1,0:T(8,128)(2,1)S(1)} %copy-done.3), channel_id=1, source_target_pairs={{0,1},{1,0},{2,3},{3,2},{4,5},{5,4},{6,7},{7,6},{8,9},{9,8},{10,11... | collective-permute-start | bytes 3932168 | tf_op jit(solution)/shard_map/ppermute | solution.py:146
  22.9 248.1 %copy-start.51 = (pred[1024]{0:T(1024)(128)(4,1)}, pred[1024]{0:T(1024)(128)(4,1)S(1)}, u32[]{:S(2)}) copy-start(pred[1024]{0:T(1024)(128)(4,1)S(1)} %iota_compare_fusion.1) | copy-start | bytes 3076
  44.4 9.7 %collective-permute-start.8 = (bf16[4,80,640]{2,1,0:T(8,128)(2,1)S(1)}, bf16[4,80,640]{2,1,0:T(8,128)(2,1)S(1)}, u32[]{:S(2)}, u32[]{:S(2)}) collective-permute-start(bf16[4,80,640]{2,1,0:T(8,128)(2,1)S(1)} %bitcast.340), channel_id=1, source_target_pairs={{0,2},{1,3},{2,0},{3,1},{4,6},{5,7},{6,4},{7,5},{8,10},{9,11},{10,... | collective-permute-start | bytes 1228808 | tf_op jit(solution)/shard_map/ppermute | solution.py:149
  45.9 10.4 %collective-permute-start.9 = (bf16[4,80,640]{2,1,0:T(8,128)(2,1)S(1)}, bf16[4,80,640]{2,1,0:T(8,128)(2,1)S(1)}, u32[]{:S(2)}, u32[]{:S(2)}) collective-permute-start(bf16[4,80,640]{2,1,0:T(8,128)(2,1)S(1)} %bitcast.341), channel_id=1, source_target_pairs={{0,4},{1,5},{2,6},{3,7},{4,0},{5,1},{6,2},{7,3},{8,12},{9,13},{10,... | collective-permute-start | bytes 1228808 | tf_op jit(solution)/shard_map/ppermute | solution.py:152
  48.2 497.4 %reduce-scatter.6.cloned.1.call-start = ((), (), s32[]{:S(2)}) async-start(), calls=%async_computation.5 | async-start | bytes 512000 | tf_op jit(solution)/shard_map/reduce_scatter | solution.py:243
  54.1 8.7 %collective-permute-start.11 = (bf16[2,80,640]{2,1,0:T(8,128)(2,1)S(1)}, bf16[2,80,640]{2,1,0:T(8,128)(2,1)S(1)}, u32[]{:S(2)}, u32[]{:S(2)}) collective-permute-start(bf16[2,80,640]{2,1,0:T(8,128)(2,1)S(1)} %slice.477), channel_id=1, source_target_pairs={{0,4},{1,5},{2,6},{3,7},{4,0},{5,1},{6,2},{7,3},{8,12},{9,13},{10,... | collective-permute-start | bytes 614408 | tf_op jit(solution)/shard_map/ppermute | solution.py:152
  56.3 5.8 collective-permute-start.10
  63.6 38.9 %collective-permute-start.12 = (bf16[1280,640]{1,0:T(8,128)(2,1)}, bf16[1280,640]{1,0:T(8,128)(2,1)}, u32[]{:S(2)}, u32[]{:S(2)}) collective-permute-start(bf16[1280,640]{1,0:T(8,128)(2,1)} %bitcast.30), channel_id=1, source_target_pairs={{0,1},{1,0},{2,3},{3,2},{4,5},{5,4},{6,7},{7,6},{8,9},{9,8},{10,11... | collective-permute-start | bytes 4915208 | tf_op jit(solution)/shard_map/ppermute | solution.py:146
  65.6 130.4 %copy-start.45 = (f32[1024]{0:T(1024)}, f32[1024]{0:T(1024)S(1)}, u32[]{:S(2)}) copy-start(f32[1024]{0:T(1024)S(1)} %broadcast_multiply_fusion.7) | copy-start | bytes 12292
  66.4 129.5 %copy-start.49 = (f32[1024]{0:T(1024)}, f32[1024]{0:T(1024)S(1)}, u32[]{:S(2)}) copy-start(f32[1024]{0:T(1024)S(1)} %add_rsqrt_fusion.1) | copy-start | bytes 12292
  70.0 67.8 %collective-permute-start.2 = (bf16[4,80,2048]{2,1,0:T(8,128)(2,1)}, bf16[4,80,2048]{2,1,0:T(8,128)(2,1)}, u32[]{:S(2)}, u32[]{:S(2)}) collective-permute-start(bf16[4,80,2048]{2,1,0:T(8,128)(2,1)} %bitcast.344), channel_id=1, source_target_pairs={{0,2},{1,3},{2,0},{3,1},{4,6},{5,7},{6,4},{7,5},{8,10},{9,11},{10,... | collective-permute-start | bytes 3932168 | tf_op jit(solution)/shard_map/ppermute | solution.py:149
  70.9 70.1 %collective-permute-start.3 = (bf16[4,80,2048]{2,1,0:T(8,128)(2,1)}, bf16[4,80,2048]{2,1,0:T(8,128)(2,1)}, u32[]{:S(2)}, u32[]{:S(2)}) collective-permute-start(bf16[4,80,2048]{2,1,0:T(8,128)(2,1)} %bitcast.345), channel_id=1, source_target_pairs={{0,4},{1,5},{2,6},{3,7},{4,0},{5,1},{6,2},{7,3},{8,12},{9,13},{10,... | collective-permute-start | bytes 3932168 | tf_op jit(solution)/shard_map/ppermute | solution.py:152
  94.9 52.9 %collective-permute-start.17 = (bf16[4,160,1280]{2,1,0:T(8,128)(2,1)}, bf16[4,160,1280]{2,1,0:T(8,128)(2,1)}, u32[]{:S(2)}, u32[]{:S(2)}) collective-permute-start(bf16[4,160,1280]{2,1,0:T(8,128)(2,1)} %bitcast.334), channel_id=1, source_target_pairs={{0,2},{1,3},{2,0},{3,1},{4,6},{5,7},{6,4},{7,5},{8,10},{9,11},{10,... | collective-permute-start | bytes 4915208 | tf_op jit(solution)/shard_map/ppermute | solution.py:149
  96.4 56.8 %collective-permute-start.18 = (bf16[4,160,1280]{2,1,0:T(8,128)(2,1)}, bf16[4,160,1280]{2,1,0:T(8,128)(2,1)}, u32[]{:S(2)}, u32[]{:S(2)}) collective-permute-start(bf16[4,160,1280]{2,1,0:T(8,128)(2,1)} %bitcast.335), channel_id=1, source_target_pairs={{0,4},{1,5},{2,6},{3,7},{4,0},{5,1},{6,2},{7,3},{8,12},{9,13},{10,... | collective-permute-start | bytes 4915208 | tf_op jit(solution)/shard_map/ppermute | solution.py:152
  134.1 91.5 %collective-permute-start.13 = (bf16[4,80,2560]{2,1,0:T(8,128)(2,1)}, bf16[4,80,2560]{2,1,0:T(8,128)(2,1)}, u32[]{:S(2)}, u32[]{:S(2)}) collective-permute-start(bf16[4,80,2560]{2,1,0:T(8,128)(2,1)} %bitcast.33), channel_id=1, source_target_pairs={{0,2},{1,3},{2,0},{3,1},{4,6},{5,7},{6,4},{7,5},{8,10},{9,11},{10,... | collective-permute-start | bytes 4915208 | tf_op jit(solution)/shard_map/ppermute | solution.py:149
  137.8 19.5 %copy-start.10 = (bf16[4,2,2,80,2560]{4,3,2,1,0:T(8,128)(2,1)}, bf16[4,2,2,80,2560]{4,3,2,1,0:T(8,128)(2,1)S(1)}, u32[]{:S(2)}) copy-start(bf16[4,2,2,80,2560]{4,3,2,1,0:T(8,128)(2,1)S(1)} %constant_dynamic-update-slice_fusion.3) | copy-start | bytes 19660804
  137.8 90.5 %collective-permute-start.14 = (bf16[4,80,2560]{2,1,0:T(8,128)(2,1)}, bf16[4,80,2560]{2,1,0:T(8,128)(2,1)}, u32[]{:S(2)}, u32[]{:S(2)}) collective-permute-start(bf16[4,80,2560]{2,1,0:T(8,128)(2,1)} %bitcast.33), channel_id=1, source_target_pairs={{0,4},{1,5},{2,6},{3,7},{4,0},{5,1},{6,2},{7,3},{8,12},{9,13},{10,... | collective-permute-start | bytes 4915208 | tf_op jit(solution)/shard_map/ppermute | solution.py:152
  141.0 49.9 %collective-permute-start.5 = (bf16[2,80,2048]{2,1,0:T(8,128)(2,1)S(1)}, bf16[2,80,2048]{2,1,0:T(8,128)(2,1)S(1)}, u32[]{:S(2)}, u32[]{:S(2)}) collective-permute-start(bf16[2,80,2048]{2,1,0:T(8,128)(2,1)S(1)} %slice.469), channel_id=1, source_target_pairs={{0,4},{1,5},{2,6},{3,7},{4,0},{5,1},{6,2},{7,3},{8,12},{9,13},{10,... | collective-permute-start | bytes 1966088 | tf_op jit(solution)/shard_map/ppermute | solution.py:152
  147.8 38.0 %collective-permute-start.4 = (bf16[2,80,2048]{2,1,0:T(8,128)(2,1)S(1)}, bf16[2,80,2048]{2,1,0:T(8,128)(2,1)S(1)}, u32[]{:S(2)}, u32[]{:S(2)}) collective-permute-start(bf16[2,80,2048]{2,1,0:T(8,128)(2,1)S(1)} %slice.468), channel_id=1, source_target_pairs={{0,2},{1,3},{2,0},{3,1},{4,6},{5,7},{6,4},{7,5},{8,10},{9,11},{10,... | collective-permute-start | bytes 1966088 | tf_op jit(solution)/shard_map/ppermute | solution.py:149
  153.2 84.5 %collective-permute-start.20 = (bf16[2,160,1280]{2,1,0:T(8,128)(2,1)}, bf16[2,160,1280]{2,1,0:T(8,128)(2,1)}, u32[]{:S(2)}, u32[]{:S(2)}) collective-permute-start(bf16[2,160,1280]{2,1,0:T(8,128)(2,1)} %slice.485), channel_id=1, source_target_pairs={{0,4},{1,5},{2,6},{3,7},{4,0},{5,1},{6,2},{7,3},{8,12},{9,13},{10,... | collective-permute-start | bytes 2457608 | tf_op jit(solution)/shard_map/ppermute | solution.py:152
  185.8 49.8 %collective-permute-start.19 = (bf16[2,160,1280]{2,1,0:T(8,128)(2,1)}, bf16[2,160,1280]{2,1,0:T(8,128)(2,1)}, u32[]{:S(2)}, u32[]{:S(2)}) collective-permute-start(bf16[2,160,1280]{2,1,0:T(8,128)(2,1)} %slice.484), channel_id=1, source_target_pairs={{0,2},{1,3},{2,0},{3,1},{4,6},{5,7},{6,4},{7,5},{8,10},{9,11},{10,... | collective-permute-start | bytes 2457608 | tf_op jit(solution)/shard_map/ppermute | solution.py:149
  225.5 26.4 %collective-permute-start.6 = (bf16[640,1024]{1,0:T(8,128)(2,1)S(1)}, bf16[640,1024]{1,0:T(8,128)(2,1)S(1)}, u32[]{:S(2)}, u32[]{:S(2)}) collective-permute-start(bf16[640,1024]{1,0:T(8,128)(2,1)S(1)} %get-tuple-element.19), channel_id=1, source_target_pairs={{0,1},{1,0},{2,3},{3,2},{4,5},{5,4},{6,7},{7,6},{8,9},{9,8},{10,11... | collective-permute-start | bytes 3932168 | tf_op jit(solution)/shard_map/ppermute | solution.py:146
  226.8 24.2 %collective-permute-start.16 = (bf16[2,80,2560]{2,1,0:T(8,128)(2,1)S(1)}, bf16[2,80,2560]{2,1,0:T(8,128)(2,1)S(1)}, u32[]{:S(2)}, u32[]{:S(2)}) collective-permute-start(bf16[2,80,2560]{2,1,0:T(8,128)(2,1)S(1)} %slice.482), channel_id=1, source_target_pairs={{0,4},{1,5},{2,6},{3,7},{4,0},{5,1},{6,2},{7,3},{8,12},{9,13},{10,... | collective-permute-start | bytes 2457608 | tf_op jit(solution)/shard_map/ppermute | solution.py:152
  229.5 20.4 %collective-permute-start.15 = (bf16[2,80,2560]{2,1,0:T(8,128)(2,1)S(1)}, bf16[2,80,2560]{2,1,0:T(8,128)(2,1)S(1)}, u32[]{:S(2)}, u32[]{:S(2)}) collective-permute-start(bf16[2,80,2560]{2,1,0:T(8,128)(2,1)S(1)} %slice.481), channel_id=1, source_target_pairs={{0,2},{1,3},{2,0},{3,1},{4,6},{5,7},{6,4},{7,5},{8,10},{9,11},{10,... | collective-permute-start | bytes 2457608 | tf_op jit(solution)/shard_map/ppermute | solution.py:149
  259.4 38.2 %copy-start.2 = (f32[1024,1280]{1,0:T(8,128)}, f32[1024,1280]{1,0:T(8,128)S(1)}, u32[]{:S(2)}) copy-start(f32[1024,1280]{1,0:T(8,128)S(1)} %get-tuple-element.117) | copy-start | bytes 15728644
  259.4 38.2 %copy-start.37 = (f32[1024]{0:T(1024)}, f32[1024]{0:T(1024)S(1)}, u32[]{:S(2)}) copy-start(f32[1024]{0:T(1024)S(1)} %broadcast_multiply_fusion.6) | copy-start | bytes 12292
  260.1 37.5 %copy-start.39 = (f32[1024]{0:T(1024)}, f32[1024]{0:T(1024)S(1)}, u32[]{:S(2)}) copy-start(f32[1024]{0:T(1024)S(1)} %add_rsqrt_fusion) | copy-start | bytes 12292
  305.6 30.6 %collective-permute-start.23 = (bf16[1024,1280]{1,0:T(8,128)(2,1)}, bf16[1024,1280]{1,0:T(8,128)(2,1)}, u32[]{:S(2)}, u32[]{:S(2)}) collective-permute-start(bf16[1024,1280]{1,0:T(8,128)(2,1)} %get-tuple-element.120), channel_id=1, source_target_pairs={{0,1},{1,0},{2,3},{3,2},{4,5},{5,4},{6,7},{7,6},{8,9},{9,8},{10,11... | collective-permute-start | bytes 7864328 | tf_op jit(solution)/shard_map/ppermute | solution.py:146
  309.1 19.9 %collective-permute-start.37 = (bf16[2,80,2560]{2,1,0:T(8,128)(2,1)}, bf16[2,80,2560]{2,1,0:T(8,128)(2,1)}, u32[]{:S(2)}, u32[]{:S(2)}) collective-permute-start(bf16[2,80,2560]{2,1,0:T(8,128)(2,1)} %get-tuple-element.56), channel_id=1, source_target_pairs={{0,4},{1,5},{2,6},{3,7},{4,0},{5,1},{6,2},{7,3},{8,12},{9,13},{10,... | collective-permute-start | bytes 2457608 | tf_op jit(solution)/shard_map/ppermute | solution.py:152
  309.6 19.6 %collective-permute-start.39 = (bf16[2,80,2560]{2,1,0:T(8,128)(2,1)}, bf16[2,80,2560]{2,1,0:T(8,128)(2,1)}, u32[]{:S(2)}, u32[]{:S(2)}) collective-permute-start(bf16[2,80,2560]{2,1,0:T(8,128)(2,1)} %get-tuple-element.57), channel_id=1, source_target_pairs={{0,2},{1,3},{2,0},{3,1},{4,6},{5,7},{6,4},{7,5},{8,10},{9,11},{10,... | collective-permute-start | bytes 2457608 | tf_op jit(solution)/shard_map/ppermute | solution.py:149
  316.1 15.4 %copy-start.17 = (bf16[2,80,2560]{2,1,0:T(8,128)(2,1)S(1)}, bf16[2,80,2560]{2,1,0:T(8,128)(2,1)}, u32[]{:S(2)}) copy-start(bf16[2,80,2560]{2,1,0:T(8,128)(2,1)} %get-tuple-element.58) | copy-start | bytes 2457604
  332.8 96.4 %collective-permute-start.40 = (bf16[4,80,2560]{2,1,0:T(8,128)(2,1)}, bf16[4,80,2560]{2,1,0:T(8,128)(2,1)}, u32[]{:S(2)}, u32[]{:S(2)}) collective-permute-start(bf16[4,80,2560]{2,1,0:T(8,128)(2,1)} %pad_maximum_fusion.7), channel_id=1, source_target_pairs={{0,4},{1,5},{2,6},{3,7},{4,0},{5,1},{6,2},{7,3},{8,12},{9,13},{10,... | collective-permute-start | bytes 4915208 | tf_op jit(solution)/shard_map/ppermute | solution.py:152
  335.6 93.6 %collective-permute-start.38 = (bf16[4,80,2560]{2,1,0:T(8,128)(2,1)}, bf16[4,80,2560]{2,1,0:T(8,128)(2,1)}, u32[]{:S(2)}, u32[]{:S(2)}) collective-permute-start(bf16[4,80,2560]{2,1,0:T(8,128)(2,1)} %pad_maximum_fusion.6), channel_id=1, source_target_pairs={{0,2},{1,3},{2,0},{3,1},{4,6},{5,7},{6,4},{7,5},{8,10},{9,11},{10,... | collective-permute-start | bytes 4915208 | tf_op jit(solution)/shard_map/ppermute | solution.py:149
  396.1 5.8 collective-permute-start.25
  396.6 5.8 collective-permute-start.27
  399.1 14.5 %collective-permute-start.24 = (bf16[512,1280]{1,0:T(8,128)(2,1)}, bf16[512,1280]{1,0:T(8,128)(2,1)}, u32[]{:S(2)}, u32[]{:S(2)}) collective-permute-start(bf16[512,1280]{1,0:T(8,128)(2,1)} %dynamic-slice_convert_fusion), channel_id=1, source_target_pairs={{0,1},{1,0},{2,3},{3,2},{4,5},{5,4},{6,7},{7,6},{8,9},{9,8},{10,11... | collective-permute-start | bytes 3932168 | tf_op jit(solution)/shard_map/ppermute | solution.py:146
  402.6 8.7 %collective-permute-start.28 = (bf16[4,80,640]{2,1,0:T(8,128)(2,1)S(1)}, bf16[4,80,640]{2,1,0:T(8,128)(2,1)S(1)}, u32[]{:S(2)}, u32[]{:S(2)}) collective-permute-start(bf16[4,80,640]{2,1,0:T(8,128)(2,1)S(1)} %pad_maximum_fusion.16), channel_id=1, source_target_pairs={{0,4},{1,5},{2,6},{3,7},{4,0},{5,1},{6,2},{7,3},{8,12},{9,13},{10,... | collective-permute-start | bytes 1228808 | tf_op jit(solution)/shard_map/ppermute | solution.py:152
  404.2 8.4 %collective-permute-start.26 = (bf16[4,80,640]{2,1,0:T(8,128)(2,1)S(1)}, bf16[4,80,640]{2,1,0:T(8,128)(2,1)S(1)}, u32[]{:S(2)}, u32[]{:S(2)}) collective-permute-start(bf16[4,80,640]{2,1,0:T(8,128)(2,1)S(1)} %pad_maximum_fusion.15), channel_id=1, source_target_pairs={{0,2},{1,3},{2,0},{3,1},{4,6},{5,7},{6,4},{7,5},{8,10},{9,11},{10,... | collective-permute-start | bytes 1228808 | tf_op jit(solution)/shard_map/ppermute | solution.py:149
  413.6 132.0 %reduce-scatter.10.cloned.1.call-start = ((), (), s32[]{:S(2)}) async-start(), calls=%async_computation.7 | async-start | bytes 102400 | tf_op jit(solution)/shard_map/reduce_scatter | solution.py:243
  418.8 4.1 collective-permute-start.33
  419.4 4.5 collective-permute-start.35
  422.9 4.5 collective-permute-start.34
  423.9 4.5 collective-permute-start.36
  429.1 116.5 %reduce-scatter.12.cloned.1.call-start = ((), (), s32[]{:S(2)}) async-start(), calls=%async_computation.8 | async-start | bytes 2048000 | tf_op jit(solution)/shard_map/reduce_scatter | solution.py:243
  433.4 112.3 %reduce-scatter.8.cloned.1.call-start = ((), (), s32[]{:S(2)}) async-start(), calls=%async_computation.6 | async-start | bytes 1536000 | tf_op jit(solution)/shard_map/reduce_scatter | solution.py:243
  443.2 13.7 %collective-permute-start.29 = (bf16[2,80,1920]{2,1,0:T(8,128)(2,1)S(1)}, bf16[2,80,1920]{2,1,0:T(8,128)(2,1)S(1)}, u32[]{:S(2)}, u32[]{:S(2)}) collective-permute-start(bf16[2,80,1920]{2,1,0:T(8,128)(2,1)S(1)} %get-tuple-element.62), channel_id=1, source_target_pairs={{0,4},{1,5},{2,6},{3,7},{4,0},{5,1},{6,2},{7,3},{8,12},{9,13},{10,... | collective-permute-start | bytes 1843208 | tf_op jit(solution)/shard_map/ppermute | solution.py:152
  444.3 12.8 %collective-permute-start.31 = (bf16[2,80,1920]{2,1,0:T(8,128)(2,1)S(1)}, bf16[2,80,1920]{2,1,0:T(8,128)(2,1)S(1)}, u32[]{:S(2)}, u32[]{:S(2)}) collective-permute-start(bf16[2,80,1920]{2,1,0:T(8,128)(2,1)S(1)} %get-tuple-element.63), channel_id=1, source_target_pairs={{0,2},{1,3},{2,0},{3,1},{4,6},{5,7},{6,4},{7,5},{8,10},{9,11},{10,... | collective-permute-start | bytes 1843208 | tf_op jit(solution)/shard_map/ppermute | solution.py:149
  454.5 22.7 %copy-start.9 = (bf16[2560,1280]{1,0:T(8,128)(2,1)}, bf16[2560,1280]{1,0:T(8,128)(2,1)S(1)}, u32[]{:S(2)}) copy-start(bf16[2560,1280]{1,0:T(8,128)(2,1)S(1)} %convolution_convert_fusion) | copy-start | bytes 19660804
  454.7 21.2 %collective-permute-start.42 = (bf16[2,160,1280]{2,1,0:T(8,128)(2,1)S(1)}, bf16[2,160,1280]{2,1,0:T(8,128)(2,1)S(1)}, u32[]{:S(2)}, u32[]{:S(2)}) collective-permute-start(bf16[2,160,1280]{2,1,0:T(8,128)(2,1)S(1)} %get-tuple-element.50), channel_id=1, source_target_pairs={{0,4},{1,5},{2,6},{3,7},{4,0},{5,1},{6,2},{7,3},{8,12},{9,13},{10,... | collective-permute-start | bytes 2457608 | tf_op jit(solution)/shard_map/ppermute | solution.py:152
  456.0 21.2 %collective-permute-start.44 = (bf16[2,160,1280]{2,1,0:T(8,128)(2,1)S(1)}, bf16[2,160,1280]{2,1,0:T(8,128)(2,1)S(1)}, u32[]{:S(2)}, u32[]{:S(2)}) collective-permute-start(bf16[2,160,1280]{2,1,0:T(8,128)(2,1)S(1)} %get-tuple-element.51), channel_id=1, source_target_pairs={{0,2},{1,3},{2,0},{3,1},{4,6},{5,7},{6,4},{7,5},{8,10},{9,11},{10,... | collective-permute-start | bytes 2457608 | tf_op jit(solution)/shard_map/ppermute | solution.py:149
  457.6 44.7 %collective-permute-start.32 = (bf16[4,80,1920]{2,1,0:T(8,128)(2,1)S(1)}, bf16[4,80,1920]{2,1,0:T(8,128)(2,1)S(1)}, u32[]{:S(2)}, u32[]{:S(2)}) collective-permute-start(bf16[4,80,1920]{2,1,0:T(8,128)(2,1)S(1)} %pad_maximum_fusion.12), channel_id=1, source_target_pairs={{0,4},{1,5},{2,6},{3,7},{4,0},{5,1},{6,2},{7,3},{8,12},{9,13},{10,... | collective-permute-start | bytes 3686408 | tf_op jit(solution)/shard_map/ppermute | solution.py:152
  459.3 44.2 %collective-permute-start.30 = (bf16[4,80,1920]{2,1,0:T(8,128)(2,1)S(1)}, bf16[4,80,1920]{2,1,0:T(8,128)(2,1)S(1)}, u32[]{:S(2)}, u32[]{:S(2)}) collective-permute-start(bf16[4,80,1920]{2,1,0:T(8,128)(2,1)S(1)} %pad_maximum_fusion.11), channel_id=1, source_target_pairs={{0,2},{1,3},{2,0},{3,1},{4,6},{5,7},{6,4},{7,5},{8,10},{9,11},{10,... | collective-permute-start | bytes 3686408 | tf_op jit(solution)/shard_map/ppermute | solution.py:149
  479.0 53.5 %collective-permute-start.45 = (bf16[4,160,1280]{2,1,0:T(8,128)(2,1)}, bf16[4,160,1280]{2,1,0:T(8,128)(2,1)S(1)}, u32[]{:S(2)}, u32[]{:S(2)}) collective-permute-start(bf16[4,160,1280]{2,1,0:T(8,128)(2,1)} %pad_maximum_fusion.9), channel_id=1, source_target_pairs={{0,4},{1,5},{2,6},{3,7},{4,0},{5,1},{6,2},{7,3},{8,12},{9,13},{10,... | collective-permute-start | bytes 4915208 | tf_op jit(solution)/shard_map/ppermute | solution.py:152
  481.2 52.4 %collective-permute-start.43 = (bf16[4,160,1280]{2,1,0:T(8,128)(2,1)}, bf16[4,160,1280]{2,1,0:T(8,128)(2,1)}, u32[]{:S(2)}, u32[]{:S(2)}) collective-permute-start(bf16[4,160,1280]{2,1,0:T(8,128)(2,1)} %pad_maximum_fusion.8), channel_id=1, source_target_pairs={{0,2},{1,3},{2,0},{3,1},{4,6},{5,7},{6,4},{7,5},{8,10},{9,11},{10,... | collective-permute-start | bytes 4915208 | tf_op jit(solution)/shard_map/ppermute | solution.py:149
  505.2 66.6 %reduce-scatter.14.cloned.1.call-start = ((), (), s32[]{:S(2)}) async-start(), calls=%async_computation.9 | async-start | bytes 2048000 | tf_op jit(solution)/shard_map/reduce_scatter | solution.py:243
  519.8 17.5 %copy-start.41 = (f32[1280]{0:T(1024)S(1)}, f32[1280]{0:T(1024)}, u32[]{:S(2)}) copy-start(f32[1280]{0:T(1024)} %get-tuple-element.101) | copy-start | bytes 15364
  519.8 17.5 %collective-permute-start.21 = (bf16[512,1280]{1,0:T(8,128)(2,1)}, bf16[512,1280]{1,0:T(8,128)(2,1)}, u32[]{:S(2)}, u32[]{:S(2)}) collective-permute-start(bf16[512,1280]{1,0:T(8,128)(2,1)} %dynamic-slice_convert_fusion.1), channel_id=1, source_target_pairs={{0,1},{1,0},{2,3},{3,2},{4,5},{5,4},{6,7},{7,6},{8,9},{9,8},{10,11... | collective-permute-start | bytes 3932168 | tf_op jit(solution)/shard_map/ppermute | solution.py:146
  546.9 26.8 %collective-permute-start.41 = (bf16[40,5248]{1,0:T(8,128)(2,1)S(1)}, bf16[40,5248]{1,0:T(8,128)(2,1)S(1)}, u32[]{:S(2)}, u32[]{:S(2)}) collective-permute-start(bf16[40,5248]{1,0:T(8,128)(2,1)S(1)} %constant_dynamic-slice_fusion), channel_id=1, source_target_pairs={{0,1},{1,0},{2,3},{3,2},{4,5},{5,4},{6,7},{7,6},{8,9},{9,8},{10,11... | collective-permute-start | bytes 1259528 | tf_op jit(solution)/shard_map/ppermute | solution.py:146
  (51 other events, 296.7 us)
Sparse Core Ops, SparseCore 0:
  14.2 41.8 all-gather.7
  57.7 37.1 all-gather.11
  97.0 37.0 all-gather.9
  413.7 18.1 reduce-scatter.5
  434.7 17.3 reduce-scatter.9
  454.3 34.4 reduce-scatter.11
  505.3 27.8 reduce-scatter.7
  537.4 34.3 reduce-scatter.13

commit v2 on v1

--- a/solution.py
+++ b/solution.py
@@ -16,6 +16,7 @@
 BF = jnp.bfloat16
 F32 = jnp.float32
 VECTORS = 128
+SMALL = pl.CostEstimate(flops=1, bytes_accessed=1, transcendentals=0)
 
 
 def contract(left, right, left_dim, right_dim):
@@ -56,11 +57,7 @@
             jax.ShapeDtypeStruct((heads, 1, rows), F32),
         ],
         compiler_params=pltpu.CompilerParams(vmem_limit_bytes=40 << 20),
-        cost_estimate=pl.CostEstimate(
-            flops=12 * width * rows * rows,
-            bytes_accessed=8 * width * rows,
-            transcendentals=heads * rows * rows,
-        ),
+        cost_estimate=SMALL,
     )(length, qkv)
 
 
@@ -109,12 +106,214 @@
         out_shape=jax.ShapeDtypeStruct((3, width, rows), BF),
         scratch_shapes=[pltpu.VMEM((HD, rows), F32), pltpu.VMEM((HD, rows), F32)],
         compiler_params=pltpu.CompilerParams(vmem_limit_bytes=48 << 20),
-        cost_estimate=pl.CostEstimate(
-            flops=22 * width * rows * rows,
-            bytes_accessed=14 * width * rows,
-            transcendentals=heads * rows * rows,
+        cost_estimate=SMALL,
+    )(length, qkv, out_grad, log_total)
+
+
+def product_kernel(left, right, out):
+    out[...] = contract(left[...], right[...], 1, 0).astype(BF)
+
+
+def product(left, right):
+    rows, depth = left.shape
+    width = right.shape[1]
+    return pl.pallas_call(
+        product_kernel,
+        grid=(width // 256,),
+        in_specs=[
+            pl.BlockSpec((rows, depth), lambda i: (0, 0), pipeline_mode=pl.Buffered(1)),
+            pl.BlockSpec((depth, 256), lambda i: (0, i)),
+        ],
+        out_specs=pl.BlockSpec((rows, 256), lambda i: (0, i)),
+        out_shape=jax.ShapeDtypeStruct((rows, width), BF),
+        compiler_params=pltpu.CompilerParams(vmem_limit_bytes=16 << 20),
+        cost_estimate=SMALL,
+    )(left, right)
+
+
+def norm_back_kernel(
+    core, mid, part, other, grad, gain, heads, attended,
+    mid_grad, attended_grad, proj_grad, gain_sum, shift_sum, branch_sum, total, held,
+):
+    at = pl.program_id(0)
+    value = mid[...]
+    center = value - jnp.mean(value, axis=-1, keepdims=True)
+    scale = lax.rsqrt(jnp.mean(center * center, axis=-1, keepdims=True) + EPS)
+    hat = center * scale
+    error = part[...].astype(F32) + other[...].astype(F32)
+    scaled = error * gain[...]
+    mean = jnp.mean(scaled, axis=-1, keepdims=True)
+    dot = jnp.mean(scaled * hat, axis=-1, keepdims=True)
+    summed = grad[...].astype(F32) + (scaled - mean - hat * dot) * scale
+    low = summed.astype(BF)
+    mid_grad[...] = summed
+    held[...] = low
+    attended_grad[...] = contract(heads[...], low, 1, 1).astype(BF)
+    side = proj_grad.shape[1]
+    columns = held[:, pl.ds(pl.multiple_of(core[0] * side, 128), side)]
+
+    @pl.when(at == 0)
+    def _():
+        total[...] = jnp.zeros_like(total)
+        gain_sum[...] = jnp.zeros_like(gain_sum)
+        shift_sum[...] = jnp.zeros_like(shift_sum)
+        branch_sum[...] = jnp.zeros_like(branch_sum)
+
+    total[...] += contract(attended[...], columns, 1, 0)
+    gain_sum[...] += jnp.sum(error * hat, axis=0, keepdims=True)
+    shift_sum[...] += jnp.sum(error, axis=0, keepdims=True)
+    branch_sum[...] += jnp.sum(low.astype(F32), axis=0, keepdims=True)
+
+    @pl.when(at == pl.num_programs(0) - 1)
+    def _():
+        proj_grad[...] = total[...].astype(BF)
+
+
+def norm_back(core, mid, part, other, grad, gain, weight, attended):
+    rows, width = mid.shape
+    side = width // 2
+    cut = 256
+    row = pl.BlockSpec((cut, width), lambda i, core: (i, 0))
+    one = pl.BlockSpec((1, width), lambda i, core: (0, 0))
+    return pl.pallas_call(
+        norm_back_kernel,
+        grid_spec=pltpu.PrefetchScalarGridSpec(
+            num_scalar_prefetch=1,
+            grid=(rows // cut,),
+            in_specs=[
+                row,
+                row,
+                row,
+                row,
+                one,
+                pl.BlockSpec((side, width), lambda i, core: (core[0], 0)),
+                pl.BlockSpec((width, cut), lambda i, core: (0, i)),
+            ],
+            out_specs=[
+                row,
+                pl.BlockSpec((side, cut), lambda i, core: (0, i)),
+                pl.BlockSpec((width, side), lambda i, core: (0, 0)),
+                one,
+                one,
+                one,
+            ],
+            scratch_shapes=[pltpu.VMEM((width, side), F32), pltpu.VMEM((cut, width), BF)],
         ),
-    )(length, qkv, out_grad, log_total)
+        out_shape=[
+            jax.ShapeDtypeStruct((rows, width), F32),
+            jax.ShapeDtypeStruct((side, rows), BF),
+            jax.ShapeDtypeStruct((width, side), BF),
+            jax.ShapeDtypeStruct((1, width), F32),
+            jax.ShapeDtypeStruct((1, width), F32),
+            jax.ShapeDtypeStruct((1, width), F32),
+        ],
+        compiler_params=pltpu.CompilerParams(vmem_limit_bytes=28 << 20),
+        cost_estimate=SMALL,
+    )(core, mid, part, other, grad, gain.reshape(1, width), weight, attended)
+
+
+def first_back_kernel(core, tokens, part, other, mid_grad, gain, grad, gain_sum, shift_sum):
+    value = tokens[...].astype(F32)
+    center = value - jnp.mean(value, axis=-1, keepdims=True)
+    scale = lax.rsqrt(jnp.mean(center * center, axis=-1, keepdims=True) + EPS)
+    hat = center * scale
+    error = part[...].astype(F32) + other[...].astype(F32)
+    scaled = error * gain[...]
+    mean = jnp.mean(scaled, axis=-1, keepdims=True)
+    dot = jnp.mean(scaled * hat, axis=-1, keepdims=True)
+    grad[...] = (mid_grad[...] + (scaled - mean - hat * dot) * scale).astype(BF)
+
+    @pl.when(pl.program_id(0) == 0)
+    def _():
+        gain_sum[...] = jnp.zeros_like(gain_sum)
+        shift_sum[...] = jnp.zeros_like(shift_sum)
+
+    gain_sum[...] += jnp.sum(error * hat, axis=0, keepdims=True)
+    shift_sum[...] += jnp.sum(error, axis=0, keepdims=True)
+
+
+def first_back(core, tokens, part, other, mid_grad, gain):
+    rows, width = tokens.shape
+    cut = 256
+    steps = rows // cut
+    own = pl.BlockSpec((cut, width), lambda i, core: (i, 0))
+    mine = pl.BlockSpec((cut, width), lambda i, core: (core[0] * steps + i, 0))
+    one = pl.BlockSpec((1, width), lambda i, core: (0, 0))
+    return pl.pallas_call(
+        first_back_kernel,
+        grid_spec=pltpu.PrefetchScalarGridSpec(
+            num_scalar_prefetch=1,
+            grid=(steps,),
+            in_specs=[own, mine, own, mine, one],
+            out_specs=[own, one, one],
+        ),
+        out_shape=[
+            jax.ShapeDtypeStruct((rows, width), BF),
+            jax.ShapeDtypeStruct((1, width), F32),
+            jax.ShapeDtypeStruct((1, width), F32),
+        ],
+        compiler_params=pltpu.CompilerParams(vmem_limit_bytes=20 << 20),
+        cost_estimate=SMALL,
+    )(core, tokens, part, other, mid_grad, gain.reshape(1, width))
+
+
+def join_kernel(plane, line, from_a, from_b, far_low, far_high, *wholes):
+    turn, at = pl.program_id(0), pl.program_id(1)
+    half = pl.num_programs(1) // 2
+
+    def put(source):
+        start = 0
+        for whole in wholes:
+            stop = start + whole.shape[-1]
+            whole[0, 0, 0] = source[0, :, start:stop]
+            start = stop
+
+    pl.when(turn == 0)(lambda: put(line))
+    pl.when(turn == 1)(lambda: put(from_a))
+    pl.when(turn == 2)(lambda: put(from_b))
+    pl.when((turn == 3) & (at < half))(lambda: put(far_low))
+    pl.when((turn == 3) & (at >= half))(lambda: put(far_high))
+
+
+def join(plane, line, near, far, cuts):
+    lines, shard, width = line.shape
+    half = lines // 2
+
+    def source(turn_of):
+        def at(turn, i, plane):
+            return (jnp.where(turn == turn_of, i, jnp.where(turn < turn_of, 0, lines - 1)), 0, 0)
+
+        return pl.BlockSpec((1, shard, width), at)
+
+    def low(turn, i, plane):
+        return (jnp.where(turn == 3, jnp.minimum(i, half - 1), 0), 0, 0)
+
+    def high(turn, i, plane):
+        return (jnp.where(turn == 3, jnp.maximum(i - half, 0), 0), 0, 0)
+
+    def target(turn, i, plane):
+        a, b = plane[0], plane[1]
+        return (i, jnp.where(turn >= 2, 1 - b, b), jnp.where(turn % 2 == 1, 1 - a, a), 0, 0)
+
+    wholes = pl.pallas_call(
+        join_kernel,
+        grid_spec=pltpu.PrefetchScalarGridSpec(
+            num_scalar_prefetch=1,
+            grid=(4, lines),
+            in_specs=[
+                source(0),
+                source(1),
+                source(2),
+                pl.BlockSpec((1, shard, width), low),
+                pl.BlockSpec((1, shard, width), high),
+            ],
+            out_specs=[pl.BlockSpec((1, 1, 1, shard, cut), target) for cut in cuts],
+        ),
+        out_shape=[jax.ShapeDtypeStruct((lines, 2, 2, shard, cut), line.dtype) for cut in cuts],
+        compiler_params=pltpu.CompilerParams(vmem_limit_bytes=24 << 20),
+        cost_estimate=SMALL,
+    )(plane, line, *near, *far)
+    return [whole.reshape(lines * 4 * shard, whole.shape[-1]) for whole in wholes]
 
 
 def make_body(devices):
@@ -182,6 +381,7 @@
         side = width // 2
         hidden = up_weight.shape[1]
         block = hidden // devices
+        part = block // 2
         spread = block // shard
         length = lax.dynamic_slice(lengths, (chip,), (1,))
 
@@ -199,45 +399,67 @@
                 weight.shape[0], chips * block
             )
 
-        def gather(value):
-            line = lax.all_gather(value, "dev", axis=0, axis_index_groups=groups)
-            from_a = swap_a(line)
-            from_b = swap_b(line)
-            far_low = swap_a(from_b[:half])
-            far_high = swap_b(from_a[half:])
-            whole = jnp.zeros((lines, 2, 2) + value.shape, value.dtype)
-            zero = jnp.int32(0)
-
-            def put(whole, part, line_at, b, a):
-                return lax.dynamic_update_slice(
-                    whole, part[:, None, None], (jnp.int32(line_at), b, a, zero, zero)
-                )
-
-            whole = put(whole, line, 0, at_b, at_a)
-            whole = put(whole, from_a, 0, at_b, 1 - at_a)
-            whole = put(whole, from_b, 0, 1 - at_b, at_a)
-            whole = put(whole, far_low, 0, 1 - at_b, 1 - at_a)
-            whole = put(whole, far_high, half, 1 - at_b, 1 - at_a)
-            return whole.reshape(chips * value.shape[0], value.shape[1])
-
-        def scatter_plane(whole):
+        def after(value, *earlier):
+            return lax.optimization_barrier((value, *earlier))[0]
+
+        def gather_line(value):
+            return lax.all_gather(value, "dev", axis=0, axis_index_groups=groups)
+
+        def gather_near(line):
+            return swap_a(line), swap_b(line)
+
+        def gather_far(near):
+            from_a, from_b = near
+            return swap_a(from_b[:half]), swap_b(from_a[half:])
+
+        plane = jnp.stack([at_a, at_b]).astype(jnp.int32)
+
+        def ordered(index, own, other):
+            return jnp.stack([jnp.where(index == 0, own, other), jnp.where(index == 0, other, own)])
+
+        def gather_plane(value):
+            value = ordered(at_a, value, swap_a(value))
+            return ordered(at_b, value, swap_b(value))
+
+        def parts_of(whole):
             parts = whole.reshape(lines, 2, 2, whole.shape[0] // chips, whole.shape[1])
 
             def pick(b, a):
                 at = lax.dynamic_index_in_dim(parts, b, 1, keepdims=False)
                 return lax.dynamic_index_in_dim(at, a, 1, keepdims=False)
 
-            far = pick(1 - at_b, 1 - at_a).astype(BF)
-            far_low = swap_a(far[:half])
-            far_high = swap_b(far[half:])
-            to_a = pick(at_b, 1 - at_a).astype(F32)
-            to_b = pick(1 - at_b, at_a).astype(F32)
-            to_a = jnp.concatenate([to_a[:half], to_a[half:] + far_high.astype(F32)], axis=0)
-            to_b = jnp.concatenate([to_b[:half] + far_low.astype(F32), to_b[half:]], axis=0)
-            from_a = swap_a(to_a.astype(BF))
-            from_b = swap_b(to_b.astype(BF))
-            own = pick(at_b, at_a).astype(F32) + from_a.astype(F32) + from_b.astype(F32)
+            return pick
+
+        def give_far(pick):
+            far = pick(1 - at_b, 1 - at_a)
+            return far[:half], far[half:]
+
+        def scatter_far(pick):
+            given = give_far(pick)
+            return swap_a(given[0]), swap_b(given[1])
+
+        def scatter_add(pick, far):
+            far_low, far_high = far
+            to_a = pick(at_b, 1 - at_a)
+            to_b = pick(1 - at_b, at_a)
+            to_a = jnp.concatenate([to_a[:half], to_a[half:] + far_high], axis=0)
+            to_b = jnp.concatenate([to_b[:half] + far_low, to_b[half:]], axis=0)
+            return to_a, to_b
+
+        def scatter_near(given):
+            return swap_a(given[0]), swap_b(given[1])
+
+        def scatter_own(pick, near):
+            own = pick(at_b, at_a).astype(F32) + near[0].astype(F32) + near[1].astype(F32)
             return own.astype(BF)
+
+        def scatter_a(parts):
+            own = lax.dynamic_index_in_dim(parts, at_a, 1, keepdims=False)
+            return own + swap_a(lax.dynamic_index_in_dim(parts, 1 - at_a, 1, keepdims=False))
+
+        def scatter_b(parts):
+            own = lax.dynamic_index_in_dim(parts, at_b, 0, keepdims=False)
+            return own + swap_b(lax.dynamic_index_in_dim(parts, 1 - at_b, 0, keepdims=False))
 
         def scatter_line(parts):
             return lax.psum_scatter(
@@ -259,34 +481,50 @@
         )
         qkv_shard = both(own_qkv, swap_core(give_qkv))
         all_tokens = both(tokens, swap_core(tokens)).astype(F32)
-        rest_own = jnp.concatenate([columns(proj_weight, core), blocks(up_weight, core)], axis=1)
-        rest_give = jnp.concatenate([columns(proj_weight, other), blocks(up_weight, other)], axis=1)
-        rest_shard = both(rest_own, swap_core(rest_give))
+        tokens, up_weight, proj_weight = lax.optimization_barrier((tokens, up_weight, proj_weight, qkv_shard))[:3]
+
+        def rest_columns(which):
+            return jnp.concatenate([columns(proj_weight, which), blocks(up_weight, which)], axis=1)
+
+        rest_shard = both(rest_columns(core), swap_core(rest_columns(other)))
         all_grad = both(out_grad, swap_core(out_grad))
         live = jnp.arange(rows) < length[0]
         grad_low = jnp.where(live[:, None], all_grad, jnp.zeros_like(all_grad))
 
-        w_qkv_wide = gather(qkv_shard)
-        w_proj_side = gather(rest_shard[:, :side])
-        w_up = gather(rest_shard[:, side:])
-        w_down = gather(down_weight)
-
-        w_qkv = w_qkv_wide[:, : 3 * side]
-        table = w_qkv_wide[:, 3 * side :].astype(F32).T
+        def put(whole, block_of, line_at, b, a):
+            zero = jnp.int32(0)
+            return lax.dynamic_update_slice(
+                whole, block_of[:, None, None], (jnp.int32(line_at), b, a, zero, zero)
+            )
+
+        qkv_line = gather_line(qkv_shard)
+        rest_line = gather_line(rest_shard)
+        down_line = gather_line(down_weight)
+        qkv_near = gather_near(qkv_line)
+        from_a, from_b = qkv_near
+        down_b_grad = 0.5 * jnp.sum(grad_low.astype(F32), axis=0)
+        from_a, from_b, grad_low, down_b_grad = lax.optimization_barrier((from_a, from_b, grad_low, down_b_grad))
+        given_far = (from_b[:half], from_a[half:])
+        qkv_far = swap_a(given_far[0]), swap_b(given_far[1])
+        rest_near = gather_near(after(rest_line, *given_far))
+        w_qkv = jnp.zeros((lines, 2, 2, 2 * shard, 3 * side + VECTORS), BF)
+        w_qkv = put(w_qkv, qkv_line, 0, at_b, at_a)
+        w_qkv = put(w_qkv, from_a, 0, at_b, 1 - at_a)
+        w_qkv = put(w_qkv, from_b, 0, 1 - at_b, at_a)
+        w_qkv = put(w_qkv, qkv_far[0], 0, 1 - at_b, 1 - at_a)
+        w_qkv = put(w_qkv, qkv_far[1], half, 1 - at_b, 1 - at_a)
+        w_qkv = w_qkv.reshape(width, 3 * side + VECTORS)
+        table = w_qkv[:, 3 * side :].astype(F32).T
+        w_qkv = w_qkv[:, : 3 * side]
         gain_one, shift_one, b_query, b_value, b_proj, gain_two, shift_two, b_down = (
             table[i] for i in range(8)
         )
         hidden_bias = table[8 : 8 + spread].reshape(spread, chips, 2, shard)
         hidden_bias = lax.dynamic_index_in_dim(hidden_bias, core, 2, keepdims=False)
         hidden_bias = hidden_bias.transpose(1, 2, 0).reshape(chips * block)
-        w_proj_other = swap_core(w_proj_side)
-        w_proj = jnp.concatenate(
-            [
-                jnp.where(core == 0, w_proj_side, w_proj_other),
-                jnp.where(core == 0, w_proj_other, w_proj_side),
-            ],
-            axis=1,
-        )
+
+        def rows_of(value, which):
+            return lax.dynamic_slice(value, (which * own_rows, 0), (own_rows, value.shape[1]))
 
         def own_side(vector):
             return lax.dynamic_slice(vector, (core * side,), (side,))
@@ -312,7 +550,20 @@
         qkv_bias = jnp.concatenate([own_side(b_query), jnp.zeros((side,), F32), own_side(b_value)])
         qkv = (contract(w_qkv, normed, 0, 1) + qkv_bias[:, None]).astype(BF).reshape(3, side, rows)
         attended_own, log_total = attend(length, qkv)
+        attended_own, down_line, *rest_near = lax.optimization_barrier((attended_own, down_line, *rest_near))
+        rest_far = gather_far(rest_near)
         attended = both(attended_own, swap_core(attended_own))
+        attended, *rest_far = lax.optimization_barrier((attended, *rest_far))
+        down_near = gather_near(after(down_line, *rest_far))
+        w_proj_side, w_up = join(plane, rest_line, rest_near, rest_far, (side, chips * block))
+        w_proj_other = swap_core(w_proj_side)
+        w_proj = jnp.concatenate(
+            [
+                jnp.where(core == 0, w_proj_side, w_proj_other),
+                jnp.where(core == 0, w_proj_other, w_proj_side),
+            ],
+            axis=1,
+        )
         mid = all_tokens + contract(attended, w_proj, 0, 0) + b_proj
         mid_normed, mid_hat, mid_scale = normalize(mid, gain_two, shift_two)
         mid_low = mid_normed.astype(BF)
@@ -320,41 +571,65 @@
         below = 0.5 + 0.5 * lax.erf(pre_act * math.sqrt(0.5))
         activ = (pre_act * below).astype(BF)
         slope = (below + pre_act * (jnp.exp(-0.5 * pre_act * pre_act) * (1.0 / math.sqrt(2.0 * math.pi)))).astype(BF)
-        down_grad = contract(activ, grad_low, 0, 0).astype(BF)
-        down_part = contract(activ, w_down, 1, 0)
-
-        def rows_of(value, which):
-            return lax.dynamic_slice(value, (which * own_rows, 0), (own_rows, value.shape[1]))
-
-        down_other = swap_core(rows_of(down_part, other).astype(BF))
-        output = (
-            rows_of(mid, core) + rows_of(down_part, core) + down_other.astype(F32) + b_down
-        ).astype(BF)
-
-        grad_full = grad_low.astype(F32)
-        down_b_grad = 0.5 * jnp.sum(grad_full, axis=0)
+        activ, slope, *down_near = lax.optimization_barrier((activ, slope, *down_near))
+        down_far = gather_far(down_near)
+
+        down_grad = contract(activ, grad_low, 0, 0).astype(BF).reshape(lines, 2, 2, 2, part, width)
+        late_line = lax.psum_scatter(
+            down_grad[:, :, :, 1], "dev", scatter_dimension=0, axis_index_groups=groups
+        )
+        down_pick = parts_of(down_grad[:, :, :, 0].reshape(chips * part, width))
+        down_back_far = scatter_far(down_pick)
+        w_down = join(plane, down_line, down_near, down_far, (width,))[0]
+        w_down = after(w_down, down_grad)
         pre_grad = (contract(grad_low, w_down, 1, 1) * slope.astype(F32)).astype(BF)
-        up_grad = contract(mid_low, pre_grad, 0, 0).astype(BF)
+        mid_part = contract(pre_grad, w_up, 1, 1).astype(BF)
+        mid_other = swap_core(mid_part)
+        down_back_far = lax.optimization_barrier((*down_back_far, mid_part))[:2]
+        down_given = scatter_add(down_pick, down_back_far)
+        down_back_near = scatter_near(down_given)
+        up_grad = contract(after(mid_low, *down_given), pre_grad, 0, 0).astype(BF)
+        up_pick = parts_of(up_grad)
+        up_give = give_far(up_pick)
+        up_far = swap_a(up_give[0]), swap_b(up_give[1])
         up_b_grad = jnp.sum(pre_grad.astype(F32), axis=0)
-        mid_part = contract(pre_grad, w_up, 1, 1)
-        mid_e = mid_part + swap_core(mid_part.astype(BF)).astype(F32)
-        mid_back, gain_two_grad, shift_two_grad = normalize_back(mid_e, mid_hat, mid_scale, gain_two)
-        mid_grad = grad_full + mid_back
-        branch = mid_grad.astype(BF)
-        branch_side = lax.dynamic_slice(branch, (0, core * side), (rows, side))
-        proj_grad = contract(attended, branch_side, 1, 0).astype(BF)
-        proj_b_grad = 0.5 * jnp.sum(branch.astype(F32), axis=0)
-        w_proj_heads = lax.dynamic_slice(w_proj, (core * side, 0), (side, width))
-        attended_grad = contract(w_proj_heads, branch, 1, 1).astype(BF)
+        mid_other, _, _ = lax.optimization_barrier((mid_other, *up_give))
+        mid_grad, attended_grad, proj_grad, *mid_sums = norm_back(
+            core.reshape(1).astype(jnp.int32), mid, mid_part, mid_other, grad_low, gain_two, w_proj, attended
+        )
+        mid_grad, attended_grad, proj_grad, *up_far = lax.optimization_barrier(
+            (mid_grad, attended_grad, proj_grad, *up_far)
+        )
+        gain_two_grad, shift_two_grad, proj_b_grad = (0.5 * item[0] for item in mid_sums)
+        up_given = scatter_add(up_pick, up_far)
+        up_near = scatter_near(up_given)
+        proj_line = lax.psum_scatter(
+            proj_grad.reshape(lines, 2, 2, 2 * shard, side), "dev", scatter_dimension=0, axis_index_groups=groups
+        )
+        attended_grad, late_line = lax.optimization_barrier(
+            (attended_grad, late_line, proj_grad, *up_given)
+        )[:2]
         qkv_back = attend_back(length, qkv, attended_grad, log_total).reshape(3 * side, rows)
+        qkv_back, *down_back_near = lax.optimization_barrier((qkv_back, *down_back_near))
+        down_own = scatter_own(down_pick, down_back_near)
+        down_sum = scatter_line(down_own)
         qkv_grad = contract(normed, qkv_back, 0, 1).astype(BF)
+        qkv_pick = parts_of(qkv_grad)
+        qkv_give = give_far(qkv_pick)
+        qkv_far = swap_a(qkv_give[0]), swap_b(qkv_give[1])
+        normed_part = contract(after(qkv_back, *qkv_give), w_qkv, 0, 1).astype(BF)
+        normed_other = swap_core(rows_of(normed_part, other))
+        normed_part, proj_line, *qkv_far = lax.optimization_barrier((normed_part, proj_line, *qkv_far))
+        qkv_given = scatter_add(qkv_pick, qkv_far)
+        qkv_near = scatter_near(qkv_given)
+        up_near = lax.optimization_barrier((*up_near, *qkv_given))[:2]
+        up_own = scatter_own(up_pick, up_near)
         qkv_b_grad = jnp.sum(qkv_back.astype(F32), axis=1)
-        normed_part = contract(qkv_back, w_qkv, 0, 1)
-        normed_other = swap_core(rows_of(normed_part, other).astype(BF))
-        normed_e = rows_of(normed_part, core) + normed_other.astype(F32)
-        _, first_hat, first_scale = normalize(tokens.astype(F32), gain_one, shift_one)
-        first_back, gain_one_grad, shift_one_grad = normalize_back(normed_e, first_hat, first_scale, gain_one)
-        input_grad = (rows_of(mid_grad, core) + first_back).astype(BF)
+        normed_part, down_sum, *_ = lax.optimization_barrier((normed_part, down_sum, up_own, *qkv_given))
+        input_grad, gain_one_grad, shift_one_grad = first_back(
+            core.reshape(1).astype(jnp.int32), tokens, normed_part, normed_other, mid_grad, gain_one
+        )
+        gain_one_grad, shift_one_grad = gain_one_grad[0], shift_one_grad[0]
 
         def on_side(vector):
             return lax.dynamic_update_slice(jnp.zeros((width,), F32), vector, (core * side,))
@@ -370,56 +645,89 @@
                 on_side(qkv_b_grad[:side]),
                 on_side(qkv_b_grad[2 * side :]),
                 proj_b_grad,
-                0.5 * gain_two_grad,
-                0.5 * shift_two_grad,
+                gain_two_grad,
+                shift_two_grad,
                 down_b_grad,
             ],
             axis=1,
         )
         sums = jnp.concatenate([sums, up_rows], axis=1)
-        sums = jnp.pad(sums, ((0, 0), (0, VECTORS - sums.shape[1])))
-
-        down_sum = scatter_line(scatter_plane(down_grad))
-        up_sum = scatter_line(scatter_plane(up_grad))
-        proj_sum = scatter_line(scatter_plane(proj_grad))
-        qkv_sum = scatter_line(scatter_plane(qkv_grad))
-        vector_sum = scatter_line(scatter_plane(sums))
+        sums = jnp.pad(sums, ((0, 0), (0, VECTORS - sums.shape[1]))).astype(BF)
+        sums = after(sums, input_grad)
+        sums = sums.reshape(lines, 2, 2, 2 * shard, VECTORS)
+
+        def pick(b, a):
+            at = lax.dynamic_index_in_dim(sums, b, 1, keepdims=False)
+            return lax.dynamic_index_in_dim(at, a, 1, keepdims=False)
+
+        def halves(parts, axis, at):
+            own = lax.dynamic_index_in_dim(parts, at, axis, keepdims=False)
+            return own, lax.dynamic_index_in_dim(parts, 1 - at, axis, keepdims=False)
+
+        vector_come = swap_a(jnp.stack([pick(at_b, 1 - at_a), pick(1 - at_b, 1 - at_a)]))
+        late_keep, late_give = halves(after(late_line, *qkv_given), 1, at_a)
+        proj_keep, proj_give = halves(after(proj_line, *qkv_given), 1, at_a)
+        late_come, proj_come = swap_a(late_give), swap_a(proj_give)
+        up_sum = scatter_line(up_own)
+        down_part = product(after(activ, up_own), w_down)
+        down_part, vector_come, late_come, proj_come = lax.optimization_barrier(
+            (down_part, vector_come, late_come, proj_come)
+        )
+        vector_near = swap_b(pick(1 - at_b, at_a) + vector_come[1])
+        late_keep, late_give = halves(late_keep + late_come, 0, at_b)
+        proj_keep, proj_give = halves(proj_keep + proj_come, 0, at_b)
+        late_come, proj_come = swap_b(late_give), swap_b(proj_give)
+        up_sum, *qkv_near = lax.optimization_barrier((up_sum, *qkv_near, late_give, proj_give))[:3]
+        vector_own = pick(at_b, at_a) + vector_come[0] + vector_near
+        own = jnp.concatenate([scatter_own(qkv_pick, qkv_near), vector_own], axis=2)
+        qkv_sum = scatter_line(own)
+        down_other = swap_core(rows_of(down_part, other))
+        late_sum = late_keep + late_come
+        proj_sum = proj_keep + proj_come
+        output = (
+            rows_of(mid, core) + rows_of(down_part, core).astype(F32) + down_other.astype(F32) + b_down
+        ).astype(BF)
 
         def finish(sum_of, which):
             return lax.dynamic_slice(sum_of, (which * shard, 0), (shard, sum_of.shape[1]))
 
-        tail = jnp.concatenate([proj_sum, qkv_sum, vector_sum, up_sum], axis=1)
-        mine = finish(tail, core)
-        theirs = swap_core(finish(tail, other))
-        left = jnp.where(core == 0, mine, theirs).astype(F32)
-        right = jnp.where(core == 0, theirs, mine).astype(F32)
-
-        def joined(start):
-            return jnp.concatenate([left[:, start : start + side], right[:, start : start + side]], axis=1)
-
-        at_vectors = 4 * side
-        vector_rows = (
-            left[:, at_vectors : at_vectors + 8 + spread] + right[:, at_vectors : at_vectors + 8 + spread]
-        )
-        at_up = at_vectors + VECTORS
+        def exchange(sum_of):
+            mine = finish(sum_of, core)
+            theirs = swap_core(finish(sum_of, other))
+            left = jnp.where(core == 0, mine, theirs).astype(F32)
+            right = jnp.where(core == 0, theirs, mine).astype(F32)
+            return left, right
+
+        proj_left, proj_right = exchange(proj_sum)
+        up_left, up_right = exchange(after(up_sum, proj_left))
         up_all = jnp.stack(
             [
-                left[:, at_up:].reshape(shard, chips, block),
-                right[:, at_up:].reshape(shard, chips, block),
+                up_left.reshape(shard, chips, block),
+                up_right.reshape(shard, chips, block),
             ],
             axis=2,
         ).reshape(shard, hidden)
+        down_sum = jnp.concatenate([down_sum, late_sum], axis=0)
+        qkv_left, qkv_right = exchange(
+            lax.optimization_barrier((qkv_sum, up_all, down_sum, output))[0]
+        )
+
+        def joined(left, right, start):
+            return jnp.concatenate([left[:, start : start + side], right[:, start : start + side]], axis=1)
+
+        at_vectors = slice(3 * side, 3 * side + 8 + spread)
+        vector_rows = qkv_left[:, at_vectors] + qkv_right[:, at_vectors]
         return (
             output,
             input_grad,
             vector_rows[:, 0],
             vector_rows[:, 1],
-            joined(side),
+            joined(qkv_left, qkv_right, 0),
             vector_rows[:, 2],
-            joined(2 * side),
-            joined(3 * side),
+            joined(qkv_left, qkv_right, side),
+            joined(qkv_left, qkv_right, 2 * side),
             vector_rows[:, 3],
-            joined(0),
+            joined(proj_left, proj_right, 0),
             vector_rows[:, 4],
             vector_rows[:, 5],
             vector_rows[:, 6],

time: 600 us -> 503 us (0.84)
  waiting for transfers between devices: 202 us -> 134 us
  Pallas kernels: 47.5 us -> 88.6 us
  matrix products: 103 us -> 78 us
  blocking collectives: 21.4 us -> 0 us
  other arithmetic: 70.1 us -> 59.8 us
  local copies, waits for them, and re-layouts: 91.3 us -> 82.2 us
    pallas_call x0 -> x5, Pallas kernels: none -> 40.8 us  [the longest x1 15.5 us: norm_back(): pl.pallas_call(norm_back_kernel, grid_spec=pltpu.PrefetchScalarGridSpec(n...]
    ppermute x18 -> x15, waiting for transfers between devices: 51.6 us -> 22.8 us  [swap_a(): return lax.ppermute(value, 'dev', a_pairs)]
    dot_general x12 -> x9, matrix products: 103 us -> 78 us  [contract(): lax.dot_general(left, right, (((left_dim,), (right_dim,)), ((), ())), pre...]
    dynamic_update_slice x20 -> x5, local copies, waits for them, and re-layouts: 31.7 us -> 7.71 us  [put(): lax.dynamic_update_slice(whole, block_of[:, None, None], (jnp.int32(line_...]
    ppermute x18 -> x15, waiting for transfers between devices: 76.8 us -> 53.9 us  [swap_b(): return lax.ppermute(value, 'dev', b_pairs)]
    all_gather x1 -> x0, blocking collectives: 21.4 us -> none  [gather(): line = lax.all_gather(value, 'dev', axis=0, axis_index_groups=groups)]
    all_gather x3, waiting for transfers between devices: 46.7 us -> 26.6 us  [gather_line(): return lax.all_gather(value, 'dev', axis=0, axis_index_groups=groups)]
    unnamed x124 -> x138, local copies, waits for them, and re-layouts: 10.7 us -> 27.3 us
  transfers between devices with their start and end apart: 54 -> 50, of which waited for: 26 -> 21; matrix products, arithmetic and copies ran while one was open for 31% -> 37% of each run, Pallas kernels for 8% -> 16%
where the time goes in v2:
time: 503 us; the launch traced here: 495 us
  waiting for transfers between devices  134 us (27%)
  Pallas kernels  88.6 us (18%)
  local copies, waits for them, and re-layouts  82.2 us (16%)
  matrix products  78 us (16%)
  other arithmetic  59.8 us (12%)
  starting transfers between devices  36.3 us (7%)
  between operations  16.1 us (3%)
    dot_general x9, matrix products, contract(): lax.dot_general(left, right, (((left_dim,), (right_dim,)), ((), ())), pre...  78 us
    ppermute x15, waiting for transfers between devices, swap_b(): return lax.ppermute(value, 'dev', b_pairs)  53.9 us
    pallas_call x1, Pallas kernels, attend_back(): pl.pallas_call(functools.partial(attend_back_kernel, step=min(512, rows))...  31.6 us
    unnamed x138, local copies, waits for them, and re-layouts  27.3 us
    all_gather x3, waiting for transfers between devices, gather_line(): return lax.all_gather(value, 'dev', axis=0, axis_index_groups=groups)  26.6 us
    reduce_scatter x3, waiting for transfers between devices, scatter_line(): lax.psum_scatter(parts, 'dev', scatter_dimension=0, axis_index_groups=gro...  26.2 us
    ppermute x15, waiting for transfers between devices, swap_a(): return lax.ppermute(value, 'dev', a_pairs)  22.8 us
    ppermute x15, starting transfers between devices, swap_b(): return lax.ppermute(value, 'dev', b_pairs)  16.9 us
  transfers between devices with their start and end apart: 50, of which 21 were waited for; matrix products, arithmetic and copies ran while one was open for 37% of the time, Pallas kernels for 16%

profile of v2, /device:TPU:0, one launch (start us, length us, event | category | flops | bytes accessed | tf_op | source)
XLA Modules:
  0.0 494.8 jit_solution(12409167207208890029)
XLA Ops:
  14.1 1.7 reshape.245
  15.9 4.1 dynamic-slice_reduce_fusion.1
  25.0 1.6 collective-permute-done
  30.0 18.7 %all-gather.7.cloned.1.call-done = bf16[320,2048]{1,0:T(8,128)(2,1)} async-done(((bf16[80,2048]{1,0:T(8,128)(2,1)}), bf16[320,2048]{1,0:T(8,128)(2,1)}) %all-gather.7.cloned.1.call-update) | async-done | bytes 1310736 | tf_op jit(solution)/shard_map/all_gather | solution.py:406
  53.1 5.0 %convert_reduce_fusion.3 = (f32[1280]{0:T(1024)S(1)}, bf16[1024,1280]{1,0:T(8,128)(2,1)}) fusion(bf16[512,1280]{1,0:T(8,128)(2,1)S(1)} %get-tuple-element.202, bf16[512,1280]{1,0:T(8,128)(2,1)S(1)} %get-tuple-element.201, pred[1024]{0:T(1024)(128)(4,1)S(1)} %iota_compare_fusion.1), kind=kLoop, calls=%fused_computation.27 | loop fusion | flops 9173760 | bytes 5249024 | tf_op jit(solution)/shard_map/reduce_sum | solution.py:505
  58.1 3.0 broadcast_in_dim.41
  62.3 16.4 %collective-permute-done.2 = bf16[4,80,2048]{2,1,0:T(8,128)(2,1)S(1)} collective-permute-done((bf16[4,80,2048]{2,1,0:T(8,128)(2,1)}, bf16[4,80,2048]{2,1,0:T(8,128)(2,1)S(1)}, u32[]{:S(2)}, u32[]{:S(2)}) %collective-permute-start.2) | collective-permute-done | bytes 1310752 | tf_op jit(solution)/shard_map/ppermute | solution.py:348
  86.3 8.0 %all-gather.11.cloned.1.call-done = bf16[320,3200]{1,0:T(8,128)(2,1)} async-done(((bf16[80,3200]{1,0:T(8,128)(2,1)}), bf16[320,3200]{1,0:T(8,128)(2,1)}) %all-gather.11.cloned.1.call-update) | async-done | bytes 2048016 | tf_op jit(solution)/shard_map/all_gather | solution.py:406
  97.2 2.0 bitcast_dynamic-update-slice_fusion.3
  99.2 2.0 bitcast_dynamic-update-slice_fusion.2
  101.2 1.7 slice.305
  102.9 1.9 copy.119
  106.7 9.0 %add_convert_fusion = bf16[1920,1024]{1,0:T(8,128)(2,1)S(1)} fusion(f32[1920]{0:T(1024)S(1)} %pad_maximum_fusion.20, bf16[1280,2048]{1,0:T(8,128)(2,1)} %bitcast.19, f32[1280]{0:T(1024)S(1)} %get-tuple-element.207, f32[1280]{0:T(1024)S(1)} %get-tuple-element.211, f32[1024]{0:T(1024)S(1)} %add_rsqrt_fusion.1, f32[1024]{0:T(1024)S(1)} %broadcast_multiply_fusion.2, ...), kind=kOutput, calls=%fused_computation.13 | convolution fusion | flops 5048893440 | bytes 11494912 | tf_op jit(solution)/shard_map/dot_general | solution.py:23
  115.8 16.3 %shard_map.305 = (bf16[640,1024]{1,0:T(8,128)(2,1)S(1)}, f32[8,1,1024]{2,1,0:T(1,128)S(1)}) custom-call(s32[1]{0:T(128)} %dynamic_slice.178.length, bf16[3,640,1024]{2,1,0:T(8,128)(2,1)S(1)} %bitcast.219), custom_call_target="tpu_custom_call" | custom-call | flops 1 | bytes 1 | tf_op jit(solution)/shard_map/pallas_call | solution.py:44
  132.1 1.9 copy-done.2
  134.0 6.9 %collective-permute-done.9.from_b = bf16[4,80,3200]{2,1,0:T(8,128)(2,1)S(1)} collective-permute-done((bf16[4,80,3200]{2,1,0:T(8,128)(2,1)}, bf16[4,80,3200]{2,1,0:T(8,128)(2,1)S(1)}, u32[]{:S(2)}, u32[]{:S(2)}) %collective-permute-start.9) | collective-permute-done | bytes 2048032 | tf_op jit(solution)/shard_map/ppermute | solution.py:351
  146.4 22.1 %collective-permute-done.12.far_high = bf16[2,80,3200]{2,1,0:T(8,128)(2,1)S(1)} collective-permute-done((bf16[2,80,3200]{2,1,0:T(8,128)(2,1)S(1)}, bf16[2,80,3200]{2,1,0:T(8,128)(2,1)S(1)}, u32[]{:S(2)}, u32[]{:S(2)}) %collective-permute-start.12) | collective-permute-done | bytes 1024032 | tf_op jit(solution)/shard_map/ppermute | solution.py:351
  168.8 8.7 %shard_map.306 = (bf16[4,2,2,80,640]{4,3,2,1,0:T(8,128)(2,1)}, bf16[4,2,2,80,2560]{4,3,2,1,0:T(8,128)(2,1)S(1)}) custom-call(s32[2]{0:T(128)S(1)} %pad_add_fusion.plane, bf16[4,80,3200]{2,1,0:T(8,128)(2,1)S(1)} %bitcast.226, bf16[4,80,3200]{2,1,0:T(8,128)(2,1)} %collective-permute-done.8.from_a, bf16[4,80,3200]{2,1,0:T(8,128)(2,1)S(1)} %copy-done.15, ...), custom_call_target="tpu_custom_call" | custom-call | flops 1 | bytes 1 | tf_op jit(solution)/shard_map/pallas_call | solution.py:298
  177.6 2.8 copy-done.25
  181.0 1.5 collective-permute-start.15
  184.2 2.2 broadcast_select_fusion.1
  186.5 4.2 fusion.46
  193.4 2.4 slice-done
  196.5 12.1 %fusion.4 = (bf16[1024,2560]{1,0:T(8,128)(2,1)}, bf16[1024,2560]{1,0:T(8,128)(2,1)S(1)}) fusion(f32[2560]{0:T(1024)S(1)} %add.406, bf16[1024,1280]{1,0:T(8,128)(2,1)S(1)} %add_convert_fusion.1, bf16[1280,2560]{1,0:T(8,128)(2,1)S(1)} %bitcast.233), kind=kOutput, calls=%fused_computation.7 | convolution fusion | flops 6742343680 | bytes 19671040 | tf_op jit(solution)/shard_map/dot_general | solution.py:23
  208.6 10.8 %collective-permute-done.15.from_b = bf16[4,160,1280]{2,1,0:T(8,128)(2,1)S(1)} collective-permute-done((bf16[4,160,1280]{2,1,0:T(8,128)(2,1)}, bf16[4,160,1280]{2,1,0:T(8,128)(2,1)S(1)}, u32[]{:S(2)}, u32[]{:S(2)}) %collective-permute-start.15) | collective-permute-done | bytes 1638432 | tf_op jit(solution)/shard_map/ppermute | solution.py:351
  224.8 7.4 %convolution_convert_fusion.1 = bf16[2560,1280]{1,0:T(8,128)(2,1)S(1)} fusion(bf16[1024,2560]{1,0:T(8,128)(2,1)S(1)} %get-tuple-element.128.left, bf16[1024,1280]{1,0:T(8,128)(2,1)S(1)} %copy-done.6), kind=kOutput, calls=%fused_computation.2 | convolution fusion | flops 6714163200 | bytes 14417920 | tf_op jit(solution)/shard_map/dot_general | solution.py:23
  232.2 3.4 slice_bitcast_fusion
  235.7 2.8 dynamic-slice_bitcast_fusion.12
  240.3 3.7 collective-permute-done.18.far_low
  244.0 1.6 collective-permute-done.19.far_high
  247.0 4.0 shard_map.307
  251.1 12.7 %convert_reduce_fusion = (bf16[2560]{0:T(1024)(128)(2,1)S(1)}, bf16[1024,2560]{1,0:T(8,128)(2,1)}) fusion(bf16[1024,2560]{1,0:T(8,128)(2,1)} %get-tuple-element.108, bf16[1024,1280]{1,0:T(8,128)(2,1)S(1)} %copy-done.6, bf16[2560,1280]{1,0:T(8,128)(2,1)S(1)} %bitcast.217), kind=kOutput, calls=%fused_computation.8 | convolution fusion | flops 6723991040 | bytes 19665920 | tf_op jit(solution)/shard_map/dot_general | solution.py:23
  263.8 10.2 %convolution_convert_fusion.3.part = bf16[1024,1280]{1,0:T(8,128)(2,1)} fusion(bf16[1024,2560]{1,0:T(8,128)(2,1)} %get-tuple-element.244, bf16[1280,2560]{1,0:T(8,128)(2,1)S(1)} %bitcast.236), kind=kOutput, calls=%fused_computation.33 | convolution fusion | flops 6712197120 | bytes 14417920 | tf_op jit(solution)/shard_map/dot_general | solution.py:23
  274.0 1.6 fusion.31
  277.6 7.4 %convolution_convert_fusion = bf16[1280,2560]{1,0:T(8,128)(2,1)S(1)} fusion(bf16[1024,1280]{1,0:T(8,128)(2,1)S(1)} %copy-done.42, bf16[1024,2560]{1,0:T(8,128)(2,1)S(1)} %bitcast.270), kind=kOutput, calls=%fused_computation.1 | convolution fusion | flops 6714163200 | bytes 14417920 | tf_op jit(solution)/shard_map/dot_general | solution.py:23
  285.0 1.7 dynamic-slice_bitcast_fusion.1
  286.7 2.6 copy-done.33
  290.9 1.6 collective-permute-start.25
  294.8 1.7 dynamic-slice_bitcast_fusion
  297.1 1.7 copy-done.7
  298.8 15.5 %shard_map.308 = (f32[1024,1280]{1,0:T(8,128)S(1)}, bf16[640,1024]{1,0:T(8,128)(2,1)S(1)}, bf16[1280,640]{1,0:T(8,128)(2,1)S(1)}, f32[1,1280]{1,0:T(1,128)S(1)},...) custom-call(s32[1]{0:T(128)} %bitcast.42.core, f32[1024,1280]{1,0:T(8,128)} %copy-done.26, ...), custom_call_target="tpu_custom_call" | custom-call | flops 1 | bytes 1 | tf_op jit(solution)/shard_map/pallas_call | solution.py:178
  314.4 2.7 fusion.28
  322.6 31.6 %shard_map.309 = bf16[3,640,1024]{2,1,0:T(8,128)(2,1)S(1)} custom-call(s32[1]{0:T(128)} %dynamic_slice.178.length, bf16[3,640,1024]{2,1,0:T(8,128)(2,1)} %bitcast.220, bf16[640,1024]{1,0:T(8,128)(2,1)S(1)} %copy-done.24, f32[8,1,1024]{2,1,0:T(1,128)S(1)} %get-tuple-element.121.log_total), custom_call_target="tpu_custom_call" | custom-call | flops 1 | bytes 1 | tf_op jit(solution)/shard_map/pallas_call | solution.py:96
  354.3 6.7 %convolution_convert_fusion.2 = bf16[1280,1920]{1,0:T(8,128)(2,1)S(1)} fusion(bf16[1920,1024]{1,0:T(8,128)(2,1)S(1)} %bitcast.221, f32[1280]{0:T(1024)S(1)} %copy-done.58, f32[1280]{0:T(1024)S(1)} %copy-done.60, f32[1024]{0:T(1024)S(1)} %add_rsqrt_fusion.1, f32[1024]{0:T(1024)S(1)} %broadcast_multiply_fusion.2, bf16[512,1280]{1,0:T(8,128)(2,1)S(1)} %copy-done.32, ...), kind=kOutput, calls=%fused_computation.17 | convolution fusion | flops 5047418880 | bytes 11487232 | tf_op jit(solution)/shard_map/dot_general | solution.py:23
  361.0 1.5 dynamic-slice_bitcast_fusion.6
  362.5 1.5 collective-permute-start.27
  365.4 8.3 %fusion.16.part = bf16[1024,1280]{1,0:T(8,128)(2,1)S(1)} fusion(bf16[1920,1024]{1,0:T(8,128)(2,1)S(1)} %bitcast.222, bf16[1280,2048]{1,0:T(8,128)(2,1)} %bitcast.19), kind=kOutput, calls=%fused_computation.32 | convolution fusion | flops 5034475520 | bytes 11468800 | tf_op jit(solution)/shard_map/dot_general | solution.py:23
  374.8 2.8 fusion.26
  377.7 2.7 convert_reduce_fusion.1
  380.6 1.8 fusion.29
  388.3 4.2 fusion.22
  392.6 7.8 %reduce-scatter.10.cloned.1.call-done = bf16[1,80,1280]{2,1,0:T(8,128)(2,1)} async-done(((bf16[4,80,1280]{2,1,0:T(8,128)(2,1)}), bf16[1,80,1280]{2,1,0:T(8,128)(2,1)}) %reduce-scatter.10.cloned.1.call-update) | async-done | bytes 204816 | tf_op jit(solution)/shard_map/reduce_scatter | solution.py:465
  400.3 2.5 copy-done.11
  404.1 4.3 shard_map.311
  413.1 2.9 copy-done.1
  416.0 2.5 copy-done.9
  418.5 8.2 %shard_map.310 = bf16[1024,1280]{1,0:T(8,128)(2,1)S(1)} custom-call(bf16[1024,2560]{1,0:T(8,128)(2,1)S(1)} %copy-done.9, bf16[2560,1280]{1,0:T(8,128)(2,1)S(1)} %bitcast.218), custom_call_target="tpu_custom_call" | custom-call | flops 1 | bytes 1 | tf_op jit(solution)/shard_map/pallas_call | solution.py:120
  429.5 1.5 collective-permute-start.37
  433.5 10.1 %collective-permute-done.36 = bf16[4,80,128]{2,1,0:T(8,128)(2,1)S(1)} collective-permute-done((bf16[4,80,128]{2,1,0:T(8,128)(2,1)S(1)}, bf16[4,80,128]{2,1,0:T(8,128)(2,1)S(1)}, u32[]{:S(2)}, u32[]{:S(2)}) %collective-permute-start.36) | collective-permute-done | bytes 81952 | tf_op jit(solution)/shard_map/ppermute | solution.py:351
  445.8 2.5 fusion.24
  452.7 3.7 add_convert_fusion.2
  457.7 1.6 maximum_convert_fusion
  459.3 2.7 reshape.268
  462.0 18.4 %reduce-scatter.14.cloned.1.call-done = bf16[1,80,2048]{2,1,0:T(8,128)(2,1)} async-done(((bf16[4,80,2048]{2,1,0:T(8,128)(2,1)}), bf16[1,80,2048]{2,1,0:T(8,128)(2,1)}) %reduce-scatter.14.cloned.1.call-update) | async-done | bytes 327696 | tf_op jit(solution)/shard_map/reduce_scatter | solution.py:465
  (336 shorter events, 99.6 us)
Async XLA Ops:
  7.2 41.5 %all-gather.7.cloned.1.call-start = ((), (), s32[]{:S(2)}) async-start(), calls=%async_computation.10 | async-start | bytes 1638400 | tf_op jit(solution)/shard_map/all_gather | solution.py:406
  10.8 1.5 collective-permute-start.1
  13.2 81.0 %all-gather.11.cloned.1.call-start = ((), (), s32[]{:S(2)}) async-start(), calls=%async_computation.12 | async-start | bytes 2560000 | tf_op jit(solution)/shard_map/all_gather | solution.py:406
  20.4 1.6 collective-permute-start.7
  22.9 111.1 %all-gather.9.cloned.1.call-start = ((), (), s32[]{:S(2)}) async-start(), calls=%async_computation.11 | async-start | bytes 2048000 | tf_op jit(solution)/shard_map/all_gather | solution.py:406
  23.0 3.7 collective-permute-start
  23.4 28.2 %collective-permute-start.4 = (bf16[512,1280]{1,0:T(8,128)(2,1)}, bf16[512,1280]{1,0:T(8,128)(2,1)}, u32[]{:S(2)}, u32[]{:S(2)}) collective-permute-start(bf16[512,1280]{1,0:T(8,128)(2,1)} %param.20), channel_id=1, source_target_pairs={{0,1},{1,0},{2,3},{3,2},{4,5},{5,4},{6,7},{7,6},{8,9},{9,8},{10,11... | collective-permute-start | bytes 3932168 | tf_op jit(solution)/shard_map/ppermute | solution.py:345
  23.6 298.9 %reduce-scatter.6.cloned.1.call-start = ((), (), s32[]{:S(2)}) async-start(), calls=%async_computation.5 | async-start | bytes 4096000 | tf_op jit(solution)/shard_map/reduce_scatter | solution.py:578
  28.1 78.6 %copy-start.27 = (bf16[512,1280]{1,0:T(8,128)(2,1)}, bf16[512,1280]{1,0:T(8,128)(2,1)S(1)}, u32[]{:S(2)}) copy-start(bf16[512,1280]{1,0:T(8,128)(2,1)S(1)} %get-tuple-element.199) | copy-start | bytes 3932164
  28.1 23.5 %copy-start.47 = (bf16[512,1280]{1,0:T(8,128)(2,1)S(1)}, bf16[512,1280]{1,0:T(8,128)(2,1)}, u32[]{:S(2)}) copy-start(bf16[512,1280]{1,0:T(8,128)(2,1)} %param.20) | copy-start | bytes 3932164
  48.7 30.1 %collective-permute-start.2 = (bf16[4,80,2048]{2,1,0:T(8,128)(2,1)}, bf16[4,80,2048]{2,1,0:T(8,128)(2,1)S(1)}, u32[]{:S(2)}, u32[]{:S(2)}) collective-permute-start(bf16[4,80,2048]{2,1,0:T(8,128)(2,1)} %bitcast.245), channel_id=1, source_target_pairs={{0,2},{1,3},{2,0},{3,1},{4,6},{5,7},{6,4},{7,5},{8,10},{9,11},{10,... | collective-permute-start | bytes 3932168 | tf_op jit(solution)/shard_map/ppermute | solution.py:348
  50.2 29.8 %collective-permute-start.3 = (bf16[4,80,2048]{2,1,0:T(8,128)(2,1)}, bf16[4,80,2048]{2,1,0:T(8,128)(2,1)S(1)}, u32[]{:S(2)}, u32[]{:S(2)}) collective-permute-start(bf16[4,80,2048]{2,1,0:T(8,128)(2,1)} %bitcast.246), channel_id=1, source_target_pairs={{0,4},{1,5},{2,6},{3,7},{4,0},{5,1},{6,2},{7,3},{8,12},{9,13},{10,... | collective-permute-start | bytes 3932168 | tf_op jit(solution)/shard_map/ppermute | solution.py:351
  81.7 15.5 %collective-permute-start.5 = (bf16[2,80,2048]{2,1,0:T(8,128)(2,1)}, bf16[2,80,2048]{2,1,0:T(8,128)(2,1)}, u32[]{:S(2)}, u32[]{:S(2)}) collective-permute-start(bf16[2,80,2048]{2,1,0:T(8,128)(2,1)} %slice.228), channel_id=1, source_target_pairs={{0,2},{1,3},{2,0},{3,1},{4,6},{5,7},{6,4},{7,5},{8,10},{9,11},{10,... | collective-permute-start | bytes 1966088 | tf_op jit(solution)/shard_map/ppermute | solution.py:348
  82.3 16.9 %collective-permute-start.6 = (bf16[2,80,2048]{2,1,0:T(8,128)(2,1)}, bf16[2,80,2048]{2,1,0:T(8,128)(2,1)}, u32[]{:S(2)}, u32[]{:S(2)}) collective-permute-start(bf16[2,80,2048]{2,1,0:T(8,128)(2,1)} %slice.229), channel_id=1, source_target_pairs={{0,4},{1,5},{2,6},{3,7},{4,0},{5,1},{6,2},{7,3},{8,12},{9,13},{10,... | collective-permute-start | bytes 1966088 | tf_op jit(solution)/shard_map/ppermute | solution.py:351
  94.3 46.6 %collective-permute-start.9 = (bf16[4,80,3200]{2,1,0:T(8,128)(2,1)}, bf16[4,80,3200]{2,1,0:T(8,128)(2,1)S(1)}, u32[]{:S(2)}, u32[]{:S(2)}) collective-permute-start(bf16[4,80,3200]{2,1,0:T(8,128)(2,1)} %bitcast.224), channel_id=1, source_target_pairs={{0,4},{1,5},{2,6},{3,7},{4,0},{5,1},{6,2},{7,3},{8,12},{9,13},{10,... | collective-permute-start | bytes 6144008 | tf_op jit(solution)/shard_map/ppermute | solution.py:351
  95.7 46.4 %collective-permute-start.8 = (bf16[4,80,3200]{2,1,0:T(8,128)(2,1)}, bf16[4,80,3200]{2,1,0:T(8,128)(2,1)}, u32[]{:S(2)}, u32[]{:S(2)}) collective-permute-start(bf16[4,80,3200]{2,1,0:T(8,128)(2,1)} %bitcast.225), channel_id=1, source_target_pairs={{0,2},{1,3},{2,0},{3,1},{4,6},{5,7},{6,4},{7,5},{8,10},{9,11},{10,... | collective-permute-start | bytes 6144008 | tf_op jit(solution)/shard_map/ppermute | solution.py:348
  142.1 3.9 collective-permute-start.10
  143.4 25.1 %collective-permute-start.12 = (bf16[2,80,3200]{2,1,0:T(8,128)(2,1)S(1)}, bf16[2,80,3200]{2,1,0:T(8,128)(2,1)S(1)}, u32[]{:S(2)}, u32[]{:S(2)}) collective-permute-start(bf16[2,80,3200]{2,1,0:T(8,128)(2,1)S(1)} %slice.237), channel_id=1, source_target_pairs={{0,4},{1,5},{2,6},{3,7},{4,0},{5,1},{6,2},{7,3},{8,12},{9,13},{10,... | collective-permute-start | bytes 3072008 | tf_op jit(solution)/shard_map/ppermute | solution.py:351
  144.4 24.4 %collective-permute-start.11 = (bf16[2,80,3200]{2,1,0:T(8,128)(2,1)S(1)}, bf16[2,80,3200]{2,1,0:T(8,128)(2,1)S(1)}, u32[]{:S(2)}, u32[]{:S(2)}) collective-permute-start(bf16[2,80,3200]{2,1,0:T(8,128)(2,1)S(1)} %slice.236), channel_id=1, source_target_pairs={{0,2},{1,3},{2,0},{3,1},{4,6},{5,7},{6,4},{7,5},{8,10},{9,11},{10,... | collective-permute-start | bytes 3072008 | tf_op jit(solution)/shard_map/ppermute | solution.py:348
  146.1 22.7 %copy-start.20 = (bf16[320,3200]{1,0:T(8,128)(2,1)S(1)}, bf16[320,3200]{1,0:T(8,128)(2,1)}, u32[]{:S(2)}) copy-start(bf16[320,3200]{1,0:T(8,128)(2,1)} %all-gather.11.cloned.1.call-done) | copy-start | bytes 6144004
  146.1 22.7 %copy-start.15 = (bf16[4,80,3200]{2,1,0:T(8,128)(2,1)S(1)}, bf16[4,80,3200]{2,1,0:T(8,128)(2,1)}, u32[]{:S(2)}) copy-start(bf16[4,80,3200]{2,1,0:T(8,128)(2,1)} %copy-done.14) | copy-start | bytes 6144004
  146.4 40.0 %copy-start.4 = (bf16[1280,1024]{1,0:T(8,128)(2,1)}, bf16[1280,1024]{1,0:T(8,128)(2,1)S(1)}, u32[]{:S(2)}) copy-start(bf16[1280,1024]{1,0:T(8,128)(2,1)S(1)} %pad_maximum_fusion.2.attended) | copy-start | bytes 7864324
  146.4 33.9 %slice-start.4 = ((f32[128,1280]{1,0:T(8,128)}), f32[4,1280]{1,0:T(4,128)S(1)}, s32[]{:S(2)}) async-start(f32[128,1280]{1,0:T(8,128)} %copy-done.50), calls=%async_computation.17 | async-start | bytes 40960 | tf_op jit(solution)/shard_map/slice | solution.py:522
  180.3 3.8 collective-permute-start.13
  181.0 38.5 %collective-permute-start.15 = (bf16[4,160,1280]{2,1,0:T(8,128)(2,1)}, bf16[4,160,1280]{2,1,0:T(8,128)(2,1)S(1)}, u32[]{:S(2)}, u32[]{:S(2)}) collective-permute-start(bf16[4,160,1280]{2,1,0:T(8,128)(2,1)} %bitcast.227), channel_id=1, source_target_pairs={{0,4},{1,5},{2,6},{3,7},{4,0},{5,1},{6,2},{7,3},{8,12},{9,13},{10,... | collective-permute-start | bytes 4915208 | tf_op jit(solution)/shard_map/ppermute | solution.py:351
  182.5 38.1 %collective-permute-start.14 = (bf16[4,160,1280]{2,1,0:T(8,128)(2,1)}, bf16[4,160,1280]{2,1,0:T(8,128)(2,1)S(1)}, u32[]{:S(2)}, u32[]{:S(2)}) collective-permute-start(bf16[4,160,1280]{2,1,0:T(8,128)(2,1)} %bitcast.228), channel_id=1, source_target_pairs={{0,2},{1,3},{2,0},{3,1},{4,6},{5,7},{6,4},{7,5},{8,10},{9,11},{10,... | collective-permute-start | bytes 4915208 | tf_op jit(solution)/shard_map/ppermute | solution.py:348
  208.6 23.6 %copy-start.8 = (bf16[1024,2560]{1,0:T(8,128)(2,1)}, bf16[1024,2560]{1,0:T(8,128)(2,1)S(1)}, u32[]{:S(2)}) copy-start(bf16[1024,2560]{1,0:T(8,128)(2,1)S(1)} %get-tuple-element.128.left) | copy-start | bytes 15728644
  222.6 21.4 %collective-permute-start.18 = (bf16[2,160,1280]{2,1,0:T(8,128)(2,1)}, bf16[2,160,1280]{2,1,0:T(8,128)(2,1)S(1)}, u32[]{:S(2)}, u32[]{:S(2)}) collective-permute-start(bf16[2,160,1280]{2,1,0:T(8,128)(2,1)} %slice.251), channel_id=1, source_target_pairs={{0,2},{1,3},{2,0},{3,1},{4,6},{5,7},{6,4},{7,5},{8,10},{9,11},{10,... | collective-permute-start | bytes 2457608 | tf_op jit(solution)/shard_map/ppermute | solution.py:348
  224.1 21.5 %collective-permute-start.19 = (bf16[2,160,1280]{2,1,0:T(8,128)(2,1)}, bf16[2,160,1280]{2,1,0:T(8,128)(2,1)}, u32[]{:S(2)}, u32[]{:S(2)}) collective-permute-start(bf16[2,160,1280]{2,1,0:T(8,128)(2,1)} %slice.252), channel_id=1, source_target_pairs={{0,4},{1,5},{2,6},{3,7},{4,0},{5,1},{6,2},{7,3},{8,12},{9,13},{10,... | collective-permute-start | bytes 2457608 | tf_op jit(solution)/shard_map/ppermute | solution.py:351
  235.7 144.8 %reduce-scatter.8.cloned.1.call-start = ((), (), s32[]{:S(2)}) async-start(), calls=%async_computation.6 | async-start | bytes 2048000 | tf_op jit(solution)/shard_map/reduce_scatter | solution.py:606
  238.5 35.4 %collective-permute-start.16 = (bf16[2,80,1280]{2,1,0:T(8,128)(2,1)}, bf16[2,80,1280]{2,1,0:T(8,128)(2,1)}, u32[]{:S(2)}, u32[]{:S(2)}) collective-permute-start(bf16[2,80,1280]{2,1,0:T(8,128)(2,1)} %get-tuple-element.192), channel_id=1, source_target_pairs={{0,2},{1,3},{2,0},{3,1},{4,6},{5,7},{6,4},{7,5},{8,10},{9,11},{10,... | collective-permute-start | bytes 1228808 | tf_op jit(solution)/shard_map/ppermute | solution.py:348
  239.1 34.9 %collective-permute-start.17 = (bf16[2,80,1280]{2,1,0:T(8,128)(2,1)}, bf16[2,80,1280]{2,1,0:T(8,128)(2,1)}, u32[]{:S(2)}, u32[]{:S(2)}) collective-permute-start(bf16[2,80,1280]{2,1,0:T(8,128)(2,1)} %get-tuple-element.194), channel_id=1, source_target_pairs={{0,4},{1,5},{2,6},{3,7},{4,0},{5,1},{6,2},{7,3},{8,12},{9,13},{10,... | collective-permute-start | bytes 1228808 | tf_op jit(solution)/shard_map/ppermute | solution.py:351
  273.9 22.6 %collective-permute-start.20 = (bf16[1024,1280]{1,0:T(8,128)(2,1)}, bf16[1024,1280]{1,0:T(8,128)(2,1)}, u32[]{:S(2)}, u32[]{:S(2)}) collective-permute-start(bf16[1024,1280]{1,0:T(8,128)(2,1)} %convolution_convert_fusion.3.part), channel_id=1, source_target_pairs={{0,1},{1,0},{2,3},{3,2},{4,5},{5,4},{6,7},{7,6},{8,9},{9,8},{10,11... | collective-permute-start | bytes 7864328 | tf_op jit(solution)/shard_map/ppermute | solution.py:345
  289.4 25.0 %collective-permute-start.21 = (bf16[2,80,2560]{2,1,0:T(8,128)(2,1)}, bf16[2,80,2560]{2,1,0:T(8,128)(2,1)}, u32[]{:S(2)}, u32[]{:S(2)}) collective-permute-start(bf16[2,80,2560]{2,1,0:T(8,128)(2,1)} %get-tuple-element.180), channel_id=1, source_target_pairs={{0,2},{1,3},{2,0},{3,1},{4,6},{5,7},{6,4},{7,5},{8,10},{9,11},{10,... | collective-permute-start | bytes 2457608 | tf_op jit(solution)/shard_map/ppermute | solution.py:348
  290.0 24.4 %collective-permute-start.22 = (bf16[2,80,2560]{2,1,0:T(8,128)(2,1)}, bf16[2,80,2560]{2,1,0:T(8,128)(2,1)}, u32[]{:S(2)}, u32[]{:S(2)}) collective-permute-start(bf16[2,80,2560]{2,1,0:T(8,128)(2,1)} %get-tuple-element.182), channel_id=1, source_target_pairs={{0,4},{1,5},{2,6},{3,7},{4,0},{5,1},{6,2},{7,3},{8,12},{9,13},{10,... | collective-permute-start | bytes 2457608 | tf_op jit(solution)/shard_map/ppermute | solution.py:351
  290.9 63.4 %collective-permute-start.25 = (bf16[4,80,1280]{2,1,0:T(8,128)(2,1)}, bf16[4,80,1280]{2,1,0:T(8,128)(2,1)}, u32[]{:S(2)}, u32[]{:S(2)}) collective-permute-start(bf16[4,80,1280]{2,1,0:T(8,128)(2,1)} %pad_maximum_fusion.8), channel_id=1, source_target_pairs={{0,2},{1,3},{2,0},{3,1},{4,6},{5,7},{6,4},{7,5},{8,10},{9,11},{10,... | collective-permute-start | bytes 2457608 | tf_op jit(solution)/shard_map/ppermute | solution.py:348
  292.5 61.8 %collective-permute-start.26 = (bf16[4,80,1280]{2,1,0:T(8,128)(2,1)}, bf16[4,80,1280]{2,1,0:T(8,128)(2,1)}, u32[]{:S(2)}, u32[]{:S(2)}) collective-permute-start(bf16[4,80,1280]{2,1,0:T(8,128)(2,1)} %pad_maximum_fusion.9), channel_id=1, source_target_pairs={{0,4},{1,5},{2,6},{3,7},{4,0},{5,1},{6,2},{7,3},{8,12},{9,13},{10,... | collective-permute-start | bytes 2457608 | tf_op jit(solution)/shard_map/ppermute | solution.py:351
  298.8 18.3 %copy-start.40 = (bf16[2,80,2560]{2,1,0:T(8,128)(2,1)S(1)}, bf16[2,80,2560]{2,1,0:T(8,128)(2,1)}, u32[]{:S(2)}) copy-start(bf16[2,80,2560]{2,1,0:T(8,128)(2,1)} %get-tuple-element.181) | copy-start | bytes 2457604
  318.5 66.3 %collective-permute-start.23 = (bf16[4,80,2560]{2,1,0:T(8,128)(2,1)}, bf16[4,80,2560]{2,1,0:T(8,128)(2,1)}, u32[]{:S(2)}, u32[]{:S(2)}) collective-permute-start(bf16[4,80,2560]{2,1,0:T(8,128)(2,1)} %pad_maximum_fusion.3), channel_id=1, source_target_pairs={{0,2},{1,3},{2,0},{3,1},{4,6},{5,7},{6,4},{7,5},{8,10},{9,11},{10,... | collective-permute-start | bytes 4915208 | tf_op jit(solution)/shard_map/ppermute | solution.py:348
  321.8 63.0 %collective-permute-start.24 = (bf16[4,80,2560]{2,1,0:T(8,128)(2,1)}, bf16[4,80,2560]{2,1,0:T(8,128)(2,1)}, u32[]{:S(2)}, u32[]{:S(2)}) collective-permute-start(bf16[4,80,2560]{2,1,0:T(8,128)(2,1)} %pad_maximum_fusion.4), channel_id=1, source_target_pairs={{0,4},{1,5},{2,6},{3,7},{4,0},{5,1},{6,2},{7,3},{8,12},{9,13},{10,... | collective-permute-start | bytes 4915208 | tf_op jit(solution)/shard_map/ppermute | solution.py:351
  322.5 77.8 %reduce-scatter.10.cloned.1.call-start = ((), (), s32[]{:S(2)}) async-start(), calls=%async_computation.7 | async-start | bytes 1024000 | tf_op jit(solution)/shard_map/reduce_scatter | solution.py:465
  322.6 31.7 %copy-start.29 = (bf16[512,1280]{1,0:T(8,128)(2,1)S(1)}, bf16[512,1280]{1,0:T(8,128)(2,1)}, u32[]{:S(2)}) copy-start(bf16[512,1280]{1,0:T(8,128)(2,1)} %copy-done.27) | copy-start | bytes 3932164
  322.6 31.7 %copy-start.32 = (bf16[512,1280]{1,0:T(8,128)(2,1)S(1)}, bf16[512,1280]{1,0:T(8,128)(2,1)}, u32[]{:S(2)}) copy-start(bf16[512,1280]{1,0:T(8,128)(2,1)} %copy-done.30) | copy-start | bytes 3932164
  322.6 31.7 %copy-start.58 = (f32[1280]{0:T(1024)S(1)}, f32[1280]{0:T(1024)}, u32[]{:S(2)}) copy-start(f32[1280]{0:T(1024)} %copy-done.57) | copy-start | bytes 15364
  322.6 31.7 %copy-start.60 = (f32[1280]{0:T(1024)S(1)}, f32[1280]{0:T(1024)}, u32[]{:S(2)}) copy-start(f32[1280]{0:T(1024)} %copy-done.59) | copy-start | bytes 15364
  362.5 18.0 %collective-permute-start.27 = (bf16[2,80,1920]{2,1,0:T(8,128)(2,1)}, bf16[2,80,1920]{2,1,0:T(8,128)(2,1)}, u32[]{:S(2)}, u32[]{:S(2)}) collective-permute-start(bf16[2,80,1920]{2,1,0:T(8,128)(2,1)} %get-tuple-element.186), channel_id=1, source_target_pairs={{0,2},{1,3},{2,0},{3,1},{4,6},{5,7},{6,4},{7,5},{8,10},{9,11},{10,... | collective-permute-start | bytes 1843208 | tf_op jit(solution)/shard_map/ppermute | solution.py:348
  364.1 16.5 %collective-permute-start.28 = (bf16[2,80,1920]{2,1,0:T(8,128)(2,1)}, bf16[2,80,1920]{2,1,0:T(8,128)(2,1)}, u32[]{:S(2)}, u32[]{:S(2)}) collective-permute-start(bf16[2,80,1920]{2,1,0:T(8,128)(2,1)} %get-tuple-element.188), channel_id=1, source_target_pairs={{0,4},{1,5},{2,6},{3,7},{4,0},{5,1},{6,2},{7,3},{8,12},{9,13},{10,... | collective-permute-start | bytes 1843208 | tf_op jit(solution)/shard_map/ppermute | solution.py:351
  374.8 25.5 %collective-permute-start.29 = (bf16[512,1280]{1,0:T(8,128)(2,1)}, bf16[512,1280]{1,0:T(8,128)(2,1)}, u32[]{:S(2)}, u32[]{:S(2)}) collective-permute-start(bf16[512,1280]{1,0:T(8,128)(2,1)} %constant_dynamic-slice_fusion.4), channel_id=1, source_target_pairs={{0,1},{1,0},{2,3},{3,2},{4,5},{5,4},{6,7},{7,6},{8,9},{9,8},{10,11... | collective-permute-start | bytes 3932168 | tf_op jit(solution)/shard_map/ppermute | solution.py:345
  377.7 68.1 %reduce-scatter.12.cloned.1.call-start = ((), (), s32[]{:S(2)}) async-start(), calls=%async_computation.8 | async-start | bytes 2048000 | tf_op jit(solution)/shard_map/reduce_scatter | solution.py:465
  385.5 41.2 %collective-permute-start.32 = (bf16[2,80,640]{2,1,0:T(8,128)(2,1)}, bf16[2,80,640]{2,1,0:T(8,128)(2,1)}, u32[]{:S(2)}, u32[]{:S(2)}) collective-permute-start(bf16[2,80,640]{2,1,0:T(8,128)(2,1)} %dynamic-slice_bitcast_fusion.20), channel_id=1, source_target_pairs={{0,2},{1,3},{2,0},{3,1},{4,6},{5,7},{6,4},{7,5},{8,10},{9,11},{10,... | collective-permute-start | bytes 614408 | tf_op jit(solution)/shard_map/ppermute | solution.py:348
  386.9 39.9 %collective-permute-start.31 = (bf16[2,80,1280]{2,1,0:T(8,128)(2,1)}, bf16[2,80,1280]{2,1,0:T(8,128)(2,1)}, u32[]{:S(2)}, u32[]{:S(2)}) collective-permute-start(bf16[2,80,1280]{2,1,0:T(8,128)(2,1)} %dynamic-slice_bitcast_fusion.18), channel_id=1, source_target_pairs={{0,2},{1,3},{2,0},{3,1},{4,6},{5,7},{6,4},{7,5},{8,10},{9,11},{10,... | collective-permute-start | bytes 1228808 | tf_op jit(solution)/shard_map/ppermute | solution.py:348
  392.5 88.0 %reduce-scatter.14.cloned.1.call-start = ((), (), s32[]{:S(2)}) async-start(), calls=%async_computation.9 | async-start | bytes 1638400 | tf_op jit(solution)/shard_map/reduce_scatter | solution.py:465
  409.6 17.1 %collective-permute-start.30 = (bf16[2,4,80,128]{3,2,1,0:T(8,128)(2,1)}, bf16[2,4,80,128]{3,2,1,0:T(8,128)(2,1)S(1)}, u32[]{:S(2)}, u32[]{:S(2)}) collective-permute-start(bf16[2,4,80,128]{3,2,1,0:T(8,128)(2,1)} %pad_maximum_fusion.19), channel_id=1, source_target_pairs={{0,2},{1,3},{2,0},{3,1},{4,6},{5,7},{6,4},{7,5},{8,10},{9,11},{10,... | collective-permute-start | bytes 491528 | tf_op jit(solution)/shard_map/ppermute | solution.py:348
  411.1 34.7 %collective-permute-start.34 = (bf16[4,80,1920]{2,1,0:T(8,128)(2,1)}, bf16[4,80,1920]{2,1,0:T(8,128)(2,1)}, u32[]{:S(2)}, u32[]{:S(2)}) collective-permute-start(bf16[4,80,1920]{2,1,0:T(8,128)(2,1)} %pad_maximum_fusion.6), channel_id=1, source_target_pairs={{0,2},{1,3},{2,0},{3,1},{4,6},{5,7},{6,4},{7,5},{8,10},{9,11},{10,... | collective-permute-start | bytes 3686408 | tf_op jit(solution)/shard_map/ppermute | solution.py:348
  411.6 34.1 %collective-permute-start.35 = (bf16[4,80,1920]{2,1,0:T(8,128)(2,1)}, bf16[4,80,1920]{2,1,0:T(8,128)(2,1)}, u32[]{:S(2)}, u32[]{:S(2)}) collective-permute-start(bf16[4,80,1920]{2,1,0:T(8,128)(2,1)} %pad_maximum_fusion.7), channel_id=1, source_target_pairs={{0,4},{1,5},{2,6},{3,7},{4,0},{5,1},{6,2},{7,3},{8,12},{9,13},{10,... | collective-permute-start | bytes 3686408 | tf_op jit(solution)/shard_map/ppermute | solution.py:351
  426.8 16.8 %copy-start.55 = (bf16[2,4,80,128]{3,2,1,0:T(8,128)(2,1)}, bf16[2,4,80,128]{3,2,1,0:T(8,128)(2,1)S(1)}, u32[]{:S(2)}) copy-start(bf16[2,4,80,128]{3,2,1,0:T(8,128)(2,1)S(1)} %collective-permute-done.30) | copy-start | bytes 491524
  428.9 14.7 %collective-permute-start.36 = (bf16[4,80,128]{2,1,0:T(8,128)(2,1)S(1)}, bf16[4,80,128]{2,1,0:T(8,128)(2,1)S(1)}, u32[]{:S(2)}, u32[]{:S(2)}) collective-permute-start(bf16[4,80,128]{2,1,0:T(8,128)(2,1)S(1)} %bitcast_add_fusion.4), channel_id=1, source_target_pairs={{0,4},{1,5},{2,6},{3,7},{4,0},{5,1},{6,2},{7,3},{8,12},{9,13},{10,... | collective-permute-start | bytes 245768 | tf_op jit(solution)/shard_map/ppermute | solution.py:351
  429.5 16.1 %collective-permute-start.37 = (bf16[80,640]{1,0:T(8,128)(2,1)S(1)}, bf16[80,640]{1,0:T(8,128)(2,1)S(1)}, u32[]{:S(2)}, u32[]{:S(2)}) collective-permute-start(bf16[80,640]{1,0:T(8,128)(2,1)S(1)} %dynamic-slice_bitcast_fusion.21), channel_id=1, source_target_pairs={{0,4},{1,5},{2,6},{3,7},{4,0},{5,1},{6,2},{7,3},{8,12},{9,13},{10,... | collective-permute-start | bytes 307208 | tf_op jit(solution)/shard_map/ppermute | solution.py:351
  431.7 18.6 %collective-permute-start.40 = (bf16[80,1280]{1,0:T(8,128)(2,1)}, bf16[80,1280]{1,0:T(8,128)(2,1)}, u32[]{:S(2)}, u32[]{:S(2)}) collective-permute-start(bf16[80,1280]{1,0:T(8,128)(2,1)} %dynamic-slice_bitcast_fusion.19), channel_id=1, source_target_pairs={{0,4},{1,5},{2,6},{3,7},{4,0},{5,1},{6,2},{7,3},{8,12},{9,13},{10,... | collective-permute-start | bytes 614408 | tf_op jit(solution)/shard_map/ppermute | solution.py:351
  443.6 9.2 %collective-permute-start.33 = (bf16[512,1280]{1,0:T(8,128)(2,1)}, bf16[512,1280]{1,0:T(8,128)(2,1)}, u32[]{:S(2)}, u32[]{:S(2)}) collective-permute-start(bf16[512,1280]{1,0:T(8,128)(2,1)} %constant_dynamic-slice_fusion.3), channel_id=1, source_target_pairs={{0,1},{1,0},{2,3},{3,2},{4,5},{5,4},{6,7},{7,6},{8,9},{9,8},{10,11... | collective-permute-start | bytes 3932168 | tf_op jit(solution)/shard_map/ppermute | solution.py:345
  445.7 3.9 collective-permute-start.38
  452.2 4.3 collective-permute-start.39
  456.5 24.9 %copy-start.54 = (bf16[1,80,1280]{2,1,0:T(8,128)(2,1)S(1)}, bf16[1,80,1280]{2,1,0:T(8,128)(2,1)}, u32[]{:S(2)}) copy-start(bf16[1,80,1280]{2,1,0:T(8,128)(2,1)} %reduce-scatter.10.cloned.1.call-done) | copy-start | bytes 614404
  481.4 1.5 collective-permute-start.41
  (55 other events, 354.9 us)
Sparse Core Ops, SparseCore 0:
  13.3 35.2 all-gather.6
  50.3 43.9 all-gather.10
  95.8 36.9 all-gather.8
  235.8 60.8 reduce-scatter.5
  322.6 35.8 reduce-scatter.7
  377.8 22.4 reduce-scatter.9
  402.7 35.5 reduce-scatter.11
  449.7 30.7 reduce-scatter.13
